TPU v7x, 512 devices: a whole 4x4x16 slice. The times are simulated.
512 devices in a mesh: grp: 2 (over y_hi), row: 32 (over z, core), col: 8 (over x, y_lo).
Axes of the slice: x: 4, y: 4 (y_hi: 2, y_lo: 2; y = y_hi * 2 + y_lo), z: 16, core: 2. Of those that a mesh axis runs over, the one named last changes fastest.
Arguments:
- queries: bfloat16 [32, 8, 8192], P('row', None, 'col'), may hold values from -160 to 160
- tree_kv: bfloat16 [32, 8, 2, 1024], P('row', None, None, 'col'), may hold values from -6 to 6
- cache: bfloat16 [32, 2, 4096, 1024], P('row', None, 'grp', 'col'), may hold values from -6 to 6
- ctx_len: int32 [32], P('row'), may hold values from 512 to 4096, as said below
- parents: int32 [32, 8], P('row'), may hold values from -1 to 6, as said below
- stream: bfloat16 [256, 8192], P('row', ('grp', 'col')), may hold values from -64 to 64
- out_weight: bfloat16 [8192, 8192], P('row', ('grp', 'col')), may hold values from -0.0625 to 0.0625
- norm_gain: float32 [8192], P(('grp', 'col')), may hold values from 0.1 to 1.9
- gate_weight: bfloat16 [8192, 28672], P(('grp', 'col'), 'row'), may hold values from -0.0625 to 0.0625
- up_weight: bfloat16 [8192, 28672], P(('grp', 'col'), 'row'), may hold values from -0.0625 to 0.0625
- down_weight: bfloat16 [28672, 8192], P('row', ('grp', 'col')), may hold values from -0.03125 to 0.03125
Outputs:
- attended: bfloat16 [256, 8192], P('row', ('grp', 'col'))
- layer_output: bfloat16 [256, 8192], P('row', ('grp', 'col'))
Inputs may be any that keep to these rules, and one draw needn't show every extreme that they name: Request r's context occupies its first ctx_len[r] cache positions; some request fills all 4096. `parents`: node 0 of each tree is its root, marked -1; node i > 0 has a parent below i.
All inputs are finite; a program needn't handle non-finite values.
Results may differ from a plain program's by a relative error of at most 0.015.
Values may be sent and summed in bfloat16 or wider, within the bound.
No kernel may reach another device: no remote copies, remote signals or barrier semaphores. Data moves between devices by JAX's collectives and lax.ppermute only.
A program may use at most 64 MiB of HBM per device.

v0:
```python
import math

import jax
import jax.numpy as jnp
from jax import lax
from jax.sharding import PartitionSpec as P

D = 8192
HD = 128


FLOOR = -1e30
EPSILON = 1e-05


def joined(x, axis, combine):
    everything = jax.tree.map(
        lambda part, kind: lax.all_gather(part.astype(kind), axis),
        x,
        jax.tree.map(lambda a: jnp.bfloat16 if a.dtype == jnp.float32 else a.dtype, x),
    )

    def take(k):
        return jax.tree.map(lambda part, own: part[k].astype(own.dtype), everything, x)

    return lax.fori_loop(
        1, lax.axis_size(axis), lambda k, so_far: combine(so_far, take(k)), take(0)
    )


def reach_table(parents):
    tree_nodes = parents.shape[1]
    node_ids = jnp.arange(tree_nodes, dtype=jnp.int32)
    parent_hot = (parents[:, :, None] == node_ids[None, None, :]).astype(jnp.float32)
    identity = jnp.eye(tree_nodes, dtype=jnp.float32)
    reached = jnp.broadcast_to(identity, parent_hot.shape)
    for repeat in range(tree_nodes):
        reached = jnp.minimum(1.0, identity + jnp.einsum("rij,rjk->rik", parent_hot, reached))
    return reached


def absorb(running, scores, usable, values):
    maxima, totals, summed = running
    masked = jnp.where(usable, scores, FLOOR)
    new_maxima = jnp.maximum(maxima, jnp.max(masked, axis=-1))
    factor = jnp.exp(maxima - new_maxima)
    weights = jnp.where(usable, jnp.exp(scores - new_maxima[..., None]), 0.0)
    totals = totals * factor + jnp.sum(weights, axis=-1)
    product = jnp.einsum(
        "rkqs,rskd->rkqd", weights.astype(jnp.bfloat16), values, preferred_element_type=jnp.float32
    )
    summed = summed * factor[..., None] + product
    return (new_maxima, totals, summed)


def combine(former, latter):
    maxima = jnp.maximum(former[0], latter[0])
    former_scale = jnp.exp(former[0] - maxima)
    latter_scale = jnp.exp(latter[0] - maxima)
    totals = former[1] * former_scale + latter[1] * latter_scale
    summed = former[2] * former_scale[..., None] + latter[2] * latter_scale[..., None]
    return (maxima, totals, summed)


def on_device(
    queries,
    tree_kv,
    cache,
    ctx_len,
    parents,
    stream,
    out_weight,
    norm_gain,
    gate_weight,
    up_weight,
    down_weight,
):
    requests = queries.shape[0]
    tree_nodes = queries.shape[1]
    kv_local = cache.shape[3] // HD
    heads_local = queries.shape[2] // HD
    group_size = heads_local // kv_local
    local_span = cache.shape[2]
    query_rows = group_size * tree_nodes
    score_scale = 1.0 / math.sqrt(HD)
    grouped = queries.reshape(requests, tree_nodes, kv_local, group_size, HD)
    grouped = grouped.transpose(0, 2, 3, 1, 4).reshape(requests, kv_local, query_rows, HD)
    first_position = lax.axis_index("grp") * local_span
    last_group = lax.axis_index("grp") == lax.axis_size("grp") - 1
    cache_keys = cache[:, 0].reshape(requests, local_span, kv_local, HD)
    cache_values = cache[:, 1].reshape(requests, local_span, kv_local, HD)
    local_limit = ctx_len - first_position
    initial = (
        jnp.full((requests, kv_local, query_rows), FLOOR, jnp.float32),
        jnp.zeros((requests, kv_local, query_rows), jnp.float32),
        jnp.zeros((requests, kv_local, query_rows, HD), jnp.float32),
    )
    scores = (
        jnp.einsum("rkqd,rskd->rkqs", grouped, cache_keys, preferred_element_type=jnp.float32)
        * score_scale
    )
    usable = (jnp.arange(local_span, dtype=jnp.int32)[None, :] < local_limit[:, None])[
        :, None, None, :
    ]
    running = absorb(initial, scores, usable, cache_values)
    tree_keys = tree_kv[:, :, 0].reshape(requests, tree_nodes, kv_local, HD)
    tree_values = tree_kv[:, :, 1].reshape(requests, tree_nodes, kv_local, HD)
    tree_scores = (
        jnp.einsum("rkqd,rnkd->rkqn", grouped, tree_keys, preferred_element_type=jnp.float32)
        * score_scale
    )
    reached = jnp.tile(reach_table(parents), (1, group_size, 1))
    tree_usable = (reached > 0.5)[:, None, :, :] & last_group
    running = absorb(running, tree_scores, tree_usable, tree_values)
    maxima, totals, summed = joined(running, "grp", combine)
    heads_out = summed / totals[..., None]
    heads_out = heads_out.reshape(requests, kv_local, group_size, tree_nodes, HD).transpose(
        0, 3, 1, 2, 4
    )
    attention_rows = heads_out.reshape(requests * tree_nodes, heads_local * HD).astype(jnp.bfloat16)
    every_head = lax.all_gather(attention_rows, "col", axis=1, tiled=True)
    head_block = lax.all_to_all(every_head, "row", split_axis=1, concat_axis=0, tiled=True)
    portion = head_block
    projected = lax.psum_scatter(
        jnp.dot(portion, out_weight, preferred_element_type=jnp.float32).astype(jnp.bfloat16),
        "row",
        scatter_dimension=0,
        tiled=True,
    ).astype(jnp.float32)
    attended = (stream.astype(jnp.float32) + projected).astype(jnp.bfloat16)
    widened = attended.astype(jnp.float32)
    squares = lax.psum(jnp.sum(widened * widened, axis=1), ("grp", "col"))
    inverse = lax.rsqrt(squares / D + EPSILON)
    normed = (widened * inverse[:, None] * norm_gain).astype(jnp.bfloat16)
    portion = lax.all_gather(normed, "row", axis=0, tiled=True)
    gate_part = jnp.dot(portion, gate_weight, preferred_element_type=jnp.float32)
    up_part = jnp.dot(portion, up_weight, preferred_element_type=jnp.float32)
    expanded = jnp.concatenate([gate_part, up_part], axis=1)
    hidden_units = gate_weight.shape[1]
    summed_units = lax.psum(expanded.astype(jnp.bfloat16), ("grp", "col")).astype(jnp.float32)
    hidden = (jax.nn.silu(summed_units[:, :hidden_units]) * summed_units[:, hidden_units:]).astype(
        jnp.bfloat16
    )
    portion = hidden
    lowered = lax.psum_scatter(
        jnp.dot(portion, down_weight, preferred_element_type=jnp.float32).astype(jnp.bfloat16),
        "row",
        scatter_dimension=0,
        tiled=True,
    ).astype(jnp.float32)
    layer_output = (widened + lowered).astype(jnp.bfloat16)
    return (attended, layer_output)


def solution(mesh):
    placed = (
        P("row", None, "col"),
        P("row", None, None, "col"),
        P("row", None, "grp", "col"),
        P("row"),
        P("row", None),
        P("row", ("grp", "col")),
        P("row", ("grp", "col")),
        P(("grp", "col")),
        P(("grp", "col"), "row"),
        P(("grp", "col"), "row"),
        P("row", ("grp", "col")),
    )
    return jax.shard_map(
        on_device,
        mesh=mesh,
        in_specs=placed,
        out_specs=(P("row", ("grp", "col")), P("row", ("grp", "col"))),
        check_vma=False,
    )
```

profile of v0, /device:TPU:12, one launch (start us, length us, event | category | flops | bytes accessed | tf_op | source)
XLA Modules:
  0.0 491.9 jit_solution(17634796774754284077)
XLA Ops:
  7.2 0.0 copy-start
  7.2 0.0 copy-start.3
  7.2 0.0 reduce-scatter.3.cloned.1.call-start
  8.0 1.0 fusion.8
  9.1 1.0 fusion.6
  10.1 1.0 fusion.4
  11.1 0.0 copy-start.2
  11.1 1.0 fusion.11
  12.2 0.1 copy.17
  12.3 0.1 and.14
  12.4 0.8 fusion.78
  13.1 0.9 select_reduce_fusion.1
  14.0 1.5 select_reduce_fusion
  15.5 0.0 copy-start.5
  15.5 0.0 copy-start.6
  15.5 5.7 %all_gather.22 = bf16[2,1,1,64]{3,2,1,0:T(2,128)(2,1)S(1)} all-gather(bf16[1,1,1,64]{3,2,1,0:T(2,128)(2,1)S(1)} %fusion.74), channel_id=1, replica_groups=mesh['grp'=2,'row'=32,'col'=8] {'grp'}, dimensions={0}, use_global_device_ids=true | all-gather | bytes 384 | tf_op jit(solution)/shard_map/all_gather | solution.py:18
  21.3 0.3 fusion.18
  21.5 5.7 %all_gather.23 = bf16[2,1,1,64]{3,2,1,0:T(2,128)(2,1)S(1)} all-gather(bf16[1,1,1,64]{3,2,1,0:T(2,128)(2,1)S(1)} %fusion.62), channel_id=1, replica_groups=mesh['grp'=2,'row'=32,'col'=8] {'grp'}, dimensions={0}, use_global_device_ids=true | all-gather | bytes 384 | tf_op jit(solution)/shard_map/all_gather | solution.py:18
  27.3 0.1 reshape.514
  27.4 0.1 reshape.515
  27.4 0.1 reshape.512
  27.5 0.1 reshape.511
  27.6 0.0 copy-done.3
  27.6 0.3 fusion
  27.9 0.0 copy-start.1
  27.9 0.2 fusion.1
  28.2 6.1 %all-gather = bf16[128,128]{1,0:T(8,128)(2,1)S(1)} all-gather(bf16[64,128]{1,0:T(8,128)(2,1)S(1)} %fusion.1), channel_id=2, replica_groups=mesh['grp'=2,'row'=32,'col'=8] {'grp'}, dimensions={0}, use_global_device_ids=true | all-gather | bytes 49152 | tf_op jit(solution)/shard_map/all_gather | solution.py:18
  34.2 0.1 fusion.34
  34.3 28.3 %all_gather.24 = bf16[8,8192]{1,0:T(8,128)(2,1)S(1)} all-gather(bf16[8,1024]{1,0:T(8,128)(2,1)S(1)} %fusion.34), channel_id=1, replica_groups=mesh['grp'=2,'row'=32,'col'=8] {'col'}, dimensions={1}, use_global_device_ids=true | all-gather | bytes 147456 | tf_op jit(solution)/shard_map/all_gather | solution.py:121
  62.6 30.9 %all_to_all.19 = bf16[8,32,256]{2,0,1:T(8,128)(2,1)S(1)} all-to-all(bf16[8,32,256]{2,0,1:T(8,128)(2,1)S(1)} %bitcast.101), channel_id=1, replica_groups=mesh['grp'=2,'row'=32,'col'=8] {'row'}, dimensions={1} | all-to-all | bytes 262144 | tf_op jit(solution)/shard_map/all_to_all | solution.py:122
  93.5 0.0 copy-done.2
  93.5 0.9 convolution_convert_fusion.3
  94.4 0.0 reduce-scatter.3.cloned.1.call-update
  94.5 0.0 all-reduce.2.cloned.1.call-start
  94.5 99.0 %reduce-scatter.3.cloned.1.call-done = bf16[8,512]{1,0:T(8,128)(2,1)} async-done(((bf16[256,512]{1,0:T(8,128)(2,1)}), bf16[8,512]{1,0:T(8,128)(2,1)}) %reduce-scatter.3.cloned.1.call-update) | async-done | bytes 8208 | tf_op jit(solution)/shard_map/reduce_scatter | solution.py:124
  193.6 0.0 copy-done.5
  193.6 0.8 fusion.28
  194.4 0.0 copy-start.4
  194.4 29.7 %psum.14 = f32[8]{0:T(128)S(1)} all-reduce(f32[8]{0:T(128)S(1)} %get-tuple-element.22), channel_id=1, replica_groups=mesh['grp'=2,'row'=32,'col'=8] {'grp','col'}, use_global_device_ids=true, to_apply=%region_6.7 | all-reduce | flops 8 | bytes 64 | tf_op jit(solution)/shard_map/psum | solution.py:132
  224.1 0.0 copy-done.6
  224.1 0.1 fusion.30
  224.2 27.7 %all_gather.25 = bf16[256,512]{1,0:T(8,128)(2,1)S(1)} all-gather(bf16[8,512]{1,0:T(8,128)(2,1)S(1)} %fusion.30), channel_id=1, replica_groups=mesh['grp'=2,'row'=32,'col'=8] {'row'}, dimensions={0}, use_global_device_ids=true | all-gather | bytes 270336 | tf_op jit(solution)/shard_map/all_gather | solution.py:135
  251.9 0.0 copy-done
  251.9 0.4 convolution_convert_fusion
  252.3 0.0 copy-done.1
  252.3 0.4 convolution_convert_fusion.1
  252.8 1.0 pad_maximum_fusion
  253.8 0.0 copy-start.7
  253.8 0.0 all-reduce.2.cloned.1.call-update
  253.8 0.0 reduce-scatter.5.cloned.1.call-start
  253.9 118.6 %all-reduce.2.cloned.1.call-done = bf16[256,1792]{1,0:T(8,128)(2,1)} async-done(((bf16[256,1792]{1,0:T(8,128)(2,1)}), bf16[256,1792]{1,0:T(8,128)(2,1)}) %all-reduce.2.cloned.1.call-update) | async-done | bytes 917520 | tf_op jit(solution)/shard_map/psum | solution.py:140
  372.5 1.3 convert_element_type.221
  373.8 0.0 copy-done.7
  373.8 1.2 convolution_convert_fusion.2
  374.9 0.0 reduce-scatter.5.cloned.1.call-update
  375.0 109.1 %reduce-scatter.5.cloned.1.call-done = bf16[8,512]{1,0:T(8,128)(2,1)} async-done(((bf16[256,512]{1,0:T(8,128)(2,1)}), bf16[8,512]{1,0:T(8,128)(2,1)}) %reduce-scatter.5.cloned.1.call-update) | async-done | bytes 8208 | tf_op jit(solution)/shard_map/reduce_scatter | solution.py:145
  484.1 0.0 copy-done.4
  484.1 1.3 fusion.31
  (9 shorter events, 0.1 us)
Async XLA Ops:
  7.2 244.7 %copy-start = (bf16[512,896]{1,0:T(8,128)(2,1)S(1)}, bf16[512,896]{1,0:T(8,128)(2,1)}, u32[]{:S(2)}) copy-start(bf16[512,896]{1,0:T(8,128)(2,1)} %param.20) | copy-start | bytes 2752516
  7.2 20.4 %copy-start.3 = (bf16[1,2,2048,128]{3,2,1,0:T(8,128)(2,1)S(1)}, bf16[1,2,2048,128]{3,2,1,0:T(8,128)(2,1)}, u32[]{:S(2)}) copy-start(bf16[1,2,2048,128]{3,2,1,0:T(8,128)(2,1)} %param.13) | copy-start | bytes 3145732
  7.2 186.4 %reduce-scatter.3.cloned.1.call-start = ((), (), s32[]{:S(2)}) async-start(), calls=%async_computation.3 | async-start | bytes 270336 | tf_op jit(solution)/shard_map/reduce_scatter | solution.py:124
  11.1 82.4 %copy-start.2 = (bf16[256,512]{1,0:T(8,128)(2,1)S(1)}, bf16[256,512]{1,0:T(8,128)(2,1)}, u32[]{:S(2)}) copy-start(bf16[256,512]{1,0:T(8,128)(2,1)} %param.17) | copy-start | bytes 786436
  15.5 178.1 %copy-start.5 = (bf16[8,512]{1,0:T(8,128)(2,1)S(1)}, bf16[8,512]{1,0:T(8,128)(2,1)}, u32[]{:S(2)}) copy-start(bf16[8,512]{1,0:T(8,128)(2,1)} %param.16) | copy-start | bytes 24580
  15.5 208.6 %copy-start.6 = (f32[512]{0:T(512)S(1)}, f32[512]{0:T(512)}, u32[]{:S(2)}) copy-start(f32[512]{0:T(512)} %param.18) | copy-start | bytes 6148
  27.9 224.4 %copy-start.1 = (bf16[512,896]{1,0:T(8,128)(2,1)S(1)}, bf16[512,896]{1,0:T(8,128)(2,1)}, u32[]{:S(2)}) copy-start(bf16[512,896]{1,0:T(8,128)(2,1)} %param.19) | copy-start | bytes 2752516
  94.5 278.0 %all-reduce.2.cloned.1.call-start = ((), (), s32[]{:S(2)}) async-start(), calls=%async_computation.4 | async-start | bytes 1835008 | tf_op jit(solution)/shard_map/psum | solution.py:140
  194.4 289.7 %copy-start.4 = (bf16[8,512]{1,0:T(8,128)(2,1)}, bf16[8,512]{1,0:T(8,128)(2,1)S(1)}, u32[]{:S(2)}) copy-start(bf16[8,512]{1,0:T(8,128)(2,1)S(1)} %get-tuple-element.23) | copy-start | bytes 24580
  253.8 120.0 %copy-start.7 = (bf16[896,512]{1,0:T(8,128)(2,1)S(1)}, bf16[896,512]{1,0:T(8,128)(2,1)}, u32[]{:S(2)}) copy-start(bf16[896,512]{1,0:T(8,128)(2,1)} %param.21) | copy-start | bytes 2752516
  253.8 230.2 %reduce-scatter.5.cloned.1.call-start = ((), (), s32[]{:S(2)}) async-start(), calls=%async_computation.5 | async-start | bytes 270336 | tf_op jit(solution)/shard_map/reduce_scatter | solution.py:145
Sparse Core Ops, SparseCore 0:
  94.6 98.9 reduce-scatter.2
  254.0 118.4 all-reduce.1
  375.5 108.5 reduce-scatter.4
where the time goes:
time: 493 us; the launch traced here: 492 us
  waiting for transfers between devices  327 us (66%)
  blocking collectives  134 us (27%)
  between operations  14.7 us (3%)
  matrix products  9.95 us (2%)
  other arithmetic  4.98 us (1%)
    psum x1, waiting for transfers between devices, on_device(): lax.psum(expanded.astype(jnp.bfloat16), ('grp', 'col')).astype(jnp.float32)  119 us
    reduce_scatter x1, waiting for transfers between devices, on_device(): lax.psum_scatter(jnp.dot(portion, down_weight, preferred_element_type=jnp...  109 us
    reduce_scatter x1, waiting for transfers between devices, on_device(): lax.psum_scatter(jnp.dot(portion, out_weight, preferred_element_type=jnp....  99 us
    all_to_all x1, blocking collectives, on_device(): lax.all_to_all(every_head, 'row', split_axis=1, concat_axis=0, tiled=True)  30.9 us
    psum x1, blocking collectives, on_device(): squares = lax.psum(jnp.sum(widened * widened, axis=1), ('grp', 'col'))  29.7 us
    all_gather x1, blocking collectives, on_device(): every_head = lax.all_gather(attention_rows, 'col', axis=1, tiled=True)  28.3 us
    all_gather x1, blocking collectives, on_device(): portion = lax.all_gather(normed, 'row', axis=0, tiled=True)  27.7 us
    all_gather x3, blocking collectives, joined(): lax.all_gather(part.astype(kind), axis)  17.5 us
  transfers between devices with their start and end apart: 3, of which 3 were waited for; matrix products, arithmetic and copies ran while one was open for 0% of the time, Pallas kernels for 0%

commit v1 on v0

v1 whole, which is shorter than its diff:
```python
import functools
import math

import jax
import jax.numpy as jnp
from jax import lax
from jax.experimental import pallas as pl
from jax.experimental.pallas import tpu as pltpu
from jax.sharding import PartitionSpec as P

D = 8192
HD = 128
FLOOR = -1e30
EPSILON = 1e-05
PLANE = ("grp", "col")
LANES = 128
VMEM = pl.BlockSpec(memory_space=pltpu.VMEM)
SMEM = pl.BlockSpec(memory_space=pltpu.SMEM)
BF = jnp.bfloat16
F32 = jnp.float32


def call(kernel, out_shape, in_specs, flops, moved, **more):
    return pl.pallas_call(
        kernel,
        out_shape=out_shape,
        in_specs=in_specs,
        out_specs=more.pop("out_specs", jax.tree.map(lambda unused: VMEM, out_shape)),
        cost_estimate=pl.CostEstimate(flops=flops, bytes_accessed=moved, transcendentals=0),
        compiler_params=pltpu.CompilerParams(vmem_limit_bytes=32 * 1024 * 1024),
        **more,
    )


def shape(*dims, kind=BF):
    return jax.ShapeDtypeStruct(dims, kind)


def attend_kernel(copies, nodes, group, limit_ref, parents_ref, q_ref, tree_ref, cache_ref, out_ref):
    span = cache_ref.shape[2]
    rows = nodes * group
    scale = 1.0 / math.sqrt(HD)
    wide = q_ref[0].astype(F32)
    q = jnp.concatenate([wide[:, h * HD : (h + 1) * HD] for h in range(group)], axis=0).astype(BF)
    contract = (((1,), (1,)), ((), ()))
    scores = lax.dot_general(q, cache_ref[0, 0], contract, preferred_element_type=F32) * scale
    position = lax.broadcasted_iota(jnp.int32, (rows, span), 1)
    scores = jnp.where(position < limit_ref[0], scores, FLOOR)

    lane = lax.broadcasted_iota(jnp.int32, (nodes, nodes), 1)
    here = lax.broadcasted_iota(jnp.int32, (nodes, nodes), 0)
    reach = jnp.zeros((nodes, nodes), jnp.int32)
    for unused in range(nodes):
        reach = jnp.where(lane == here, 1, reach)
        above = jnp.full((nodes, nodes), -1, jnp.int32)
        for j in range(nodes):
            above = jnp.where(here == j, parents_ref[0, j], above)
        here = above
    reach = reach * limit_ref[1]
    reach = jnp.concatenate([reach] * group, axis=0)
    tree_keys = tree_ref[:, :HD]
    tree_values = tree_ref[:, HD:].astype(F32)
    tree_scores = lax.dot_general(q, tree_keys, contract, preferred_element_type=F32) * scale
    tree_scores = jnp.where(reach > 0, tree_scores, FLOOR)

    maxima = jnp.maximum(
        jnp.max(scores, axis=1, keepdims=True), jnp.max(tree_scores, axis=1, keepdims=True)
    )
    weights = jnp.exp(scores - maxima)
    tree_weights = jnp.exp(tree_scores - maxima)
    totals = jnp.sum(weights, axis=1, keepdims=True) + jnp.sum(tree_weights, axis=1, keepdims=True)
    summed = jnp.dot(weights.astype(BF), cache_ref[0, 1], preferred_element_type=F32)
    tree_rounded = tree_weights.astype(BF).astype(F32)
    for j in range(nodes):
        summed = summed + tree_rounded[:, j : j + 1] * tree_values[j : j + 1, :]
    heads = summed / totals
    level = maxima + jnp.log(totals)

    high = level.astype(BF).astype(F32)
    middle = (level - high).astype(BF).astype(F32)
    low = level - high - middle
    lanes = lax.broadcasted_iota(jnp.int32, (nodes, LANES), 1)
    tail = jnp.zeros((nodes, LANES), F32)
    for h in range(group):
        for k, part in enumerate((high, middle, low)):
            tail = jnp.where(lanes == k * group + h, part[h * nodes : (h + 1) * nodes], tail)
    line = jnp.concatenate(
        [heads[h * nodes : (h + 1) * nodes] for h in range(group)] + [tail], axis=1
    ).astype(BF)
    for k in range(copies):
        out_ref[k] = line


def join_kernel(cols, group, odd_ref, in_ref, out_ref):
    width = group * HD
    odd = odd_ref[0] > 0
    per_block = out_ref.shape[2] // HD
    block = []
    for c in range(cols):
        levels = []
        for g in range(2):
            tail = in_ref[g * cols + c, :, width:].astype(F32)
            levels.append(
                tail + jnp.roll(tail, -group, axis=1) + jnp.roll(tail, -2 * group, axis=1)
            )
        share = 1.0 / (1.0 + jnp.exp(levels[1] - levels[0]))
        rest = 1.0 / (1.0 + jnp.exp(levels[0] - levels[1]))
        for h in range(group):
            near = in_ref[c, :, h * HD : (h + 1) * HD].astype(F32)
            far = in_ref[cols + c, :, h * HD : (h + 1) * HD].astype(F32)
            block.append(near * share[:, h : h + 1] + far * rest[:, h : h + 1])
            if len(block) == per_block:
                half = per_block // 2
                first = jnp.concatenate(block[:half], axis=1)
                second = jnp.concatenate(block[half:], axis=1)
                mine = jnp.where(odd, second, first)
                other = jnp.where(odd, first, second)
                number = (c * group + h) // per_block
                out_ref[number] = jnp.concatenate([mine, other], axis=1).astype(BF)
                block = []


def project_kernel(a_ref, mine_ref, other_ref, out_ref):
    half = mine_ref.shape[0]
    out_ref[...] = (
        jnp.dot(a_ref[:, :half], mine_ref[...], preferred_element_type=F32)
        + jnp.dot(a_ref[:, half:], other_ref[...], preferred_element_type=F32)
    ).astype(BF)


def total(parts_ref):
    summed = parts_ref[0].astype(F32)
    for k in range(1, parts_ref.shape[0]):
        summed = summed + parts_ref[k].astype(F32)
    return summed


def residual_kernel(parts_ref, stream_ref, out_ref, copies_ref):
    attended = (stream_ref[...].astype(F32) + total(parts_ref)).astype(BF)
    out_ref[...] = attended
    for k in range(copies_ref.shape[0]):
        copies_ref[k] = attended


def final_kernel(parts_ref, attended_ref, out_ref):
    out_ref[...] = (attended_ref[...].astype(F32) + total(parts_ref)).astype(BF)


def widen_kernel(x_ref, gain_ref, gate_ref, up_ref, *rest):
    out_ref = rest[-1]
    units = gate_ref.shape[1]
    x = x_ref[...].astype(F32)
    squares = jnp.sum(x * x, axis=1, keepdims=True)
    scaled = (x * gain_ref[...]).astype(BF)
    out_ref[:, :units] = jnp.dot(scaled, gate_ref[...], preferred_element_type=F32).astype(BF)
    out_ref[:, units : 2 * units] = jnp.dot(
        scaled, up_ref[...], preferred_element_type=F32
    ).astype(BF)
    high = squares.astype(BF).astype(F32)
    lanes = lax.broadcasted_iota(jnp.int32, (x.shape[0], LANES), 1)
    tail = jnp.where(lanes == 0, high, jnp.where(lanes == 1, squares - high, 0.0))
    out_ref[:, 2 * units :] = tail.astype(BF)


def hidden_kernel(units, parts_ref, out_ref):
    sources = parts_ref.shape[0]

    def summed(start, size):
        return functools.reduce(
            lambda a, b: a + b,
            [parts_ref[k, :, start : start + size].astype(F32) for k in range(sources)],
        )

    squares = jnp.sum(summed(2 * units, LANES), axis=1, keepdims=True)
    inverse = lax.rsqrt(squares / D + EPSILON)
    for start in range(0, units, LANES):
        gate = summed(start, LANES) * inverse
        upward = summed(units + start, LANES) * inverse
        hidden = (gate / (1.0 + jnp.exp(-gate)) * upward).astype(BF)
        for k in range(out_ref.shape[0]):
            out_ref[k, :, start : start + LANES] = hidden


def lower_kernel(h_ref, weight_ref, out_ref):
    out_ref[...] = jnp.dot(h_ref[...], weight_ref[...], preferred_element_type=F32).astype(BF)


def lower_add_kernel(h_ref, weight_ref, other_ref, out_ref):
    out_ref[...] = (
        jnp.dot(h_ref[...], weight_ref[...], preferred_element_type=F32)
        + other_ref[...].astype(F32)
    ).astype(BF)


def on_device(
    queries,
    tree_kv,
    cache,
    ctx_len,
    parents,
    stream,
    out_weight,
    norm_gain,
    gate_weight,
    up_weight,
    down_weight,
):
    rows = lax.axis_size("row")
    cols = lax.axis_size("col")
    plane = lax.axis_size("grp") * cols
    chips = rows // 2
    ring = [[2 * z + core for z in range(chips)] for core in range(2)]
    swap = [(r, r ^ 1) for r in range(rows)]
    nodes = queries.shape[1]
    group = queries.shape[2] // HD
    span = cache.shape[2]
    local = out_weight.shape[1]
    units = gate_weight.shape[1]
    odd = (lax.axis_index("row") % 2).astype(jnp.int32).reshape(1)

    def swapped(x):
        return lax.ppermute(x, "row", swap)

    def along_ring(x):
        return lax.all_to_all(x, "row", 0, 0, axis_index_groups=ring, tiled=True)

    def in_plane(x):
        return lax.all_to_all(x, PLANE, 0, 0, tiled=True)

    other_weight = swapped(out_weight)

    last = lax.axis_index("grp") == lax.axis_size("grp") - 1
    limit = jnp.stack([ctx_len[0] - lax.axis_index("grp") * span, last.astype(jnp.int32)])
    tree = tree_kv.reshape(nodes, 2 * HD)
    width = group * HD
    lines = call(
        functools.partial(attend_kernel, plane, nodes, group),
        shape(plane, nodes, width + LANES),
        [SMEM, SMEM, VMEM, VMEM, VMEM],
        4 * nodes * group * span * HD,
        cache.size * 2,
    )(limit.astype(jnp.int32), parents, queries, tree, cache)
    lines = in_plane(lines)
    blocks = call(
        functools.partial(join_kernel, cols, group),
        shape(chips, nodes, D // chips),
        [SMEM, VMEM],
        4 * lines.size,
        lines.size * 2,
    )(odd, lines)
    tokens = chips * nodes
    portion = along_ring(blocks).reshape(tokens, D // chips)
    partial = call(
        project_kernel,
        shape(tokens, local),
        [VMEM, VMEM, VMEM],
        2 * tokens * local * (D // chips),
        out_weight.size * 4,
    )(portion, out_weight, other_weight)
    parts = along_ring(partial.reshape(chips, nodes, local))
    attended, copies = call(
        residual_kernel,
        (shape(nodes, local), shape(chips, nodes, local)),
        [VMEM, VMEM],
        parts.size,
        parts.size * 4,
    )(parts, stream)

    mine = along_ring(copies).reshape(tokens, local)
    other = swapped(mine)
    gain = norm_gain.reshape(1, local)
    wide = 2 * units + LANES
    flops = 4 * tokens * local * units
    first = call(
        widen_kernel,
        shape(2 * tokens, wide),
        [VMEM, VMEM, VMEM, VMEM],
        flops,
        gate_weight.size * 4,
        out_specs=pl.BlockSpec((tokens, wide), lambda i: (0, 0)),
        grid=(1,),
    )(mine, gain, gate_weight, up_weight)
    expanded = call(
        widen_kernel,
        shape(2 * tokens, wide),
        [VMEM, VMEM, VMEM, VMEM, pl.BlockSpec(memory_space=pl.ANY)],
        flops,
        gate_weight.size * 4,
        out_specs=pl.BlockSpec((tokens, wide), lambda i: (1, 0)),
        grid=(1,),
        input_output_aliases={4: 0},
    )(other, gain, gate_weight, up_weight, first)
    share = 2 * tokens // plane
    gathered = in_plane(expanded.reshape(plane, share, wide))
    hidden = call(
        functools.partial(hidden_kernel, units),
        shape(plane, share, units),
        [VMEM],
        gathered.size,
        gathered.size * 2,
    )(gathered)
    hidden = in_plane(hidden).reshape(2 * tokens, units)

    flops = 2 * tokens * local * units
    whole = pl.BlockSpec(down_weight.shape, lambda i: (0, 0))
    theirs = call(
        lower_kernel,
        shape(tokens, local),
        [pl.BlockSpec((tokens, units), lambda i: (1, 0)), whole],
        flops,
        down_weight.size * 2,
        grid=(1,),
        out_specs=pl.BlockSpec((tokens, local), lambda i: (0, 0)),
    )(hidden, down_weight)
    received = swapped(theirs)
    lowered = call(
        lower_add_kernel,
        shape(tokens, local),
        [
            pl.BlockSpec((tokens, units), lambda i: (0, 0)),
            whole,
            pl.BlockSpec((tokens, local), lambda i: (0, 0)),
        ],
        flops,
        down_weight.size * 2,
        grid=(1,),
        out_specs=pl.BlockSpec((tokens, local), lambda i: (0, 0)),
    )(hidden, down_weight, received)
    parts = along_ring(lowered.reshape(chips, nodes, local))
    layer_output = call(
        final_kernel, shape(nodes, local), [VMEM, VMEM], parts.size, parts.size * 2
    )(parts, attended)
    return (attended, layer_output)


def solution(mesh):
    placed = (
        P("row", None, "col"),
        P("row", None, None, "col"),
        P("row", None, "grp", "col"),
        P("row"),
        P("row", None),
        P("row", ("grp", "col")),
        P("row", ("grp", "col")),
        P(("grp", "col")),
        P(("grp", "col"), "row"),
        P(("grp", "col"), "row"),
        P("row", ("grp", "col")),
    )
    return jax.shard_map(
        on_device,
        mesh=mesh,
        in_specs=placed,
        out_specs=(P("row", ("grp", "col")), P("row", ("grp", "col"))),
        check_vma=False,
    )
```

time: 493 us -> 146 us (0.30)
  the two profiles are of different devices: /device:TPU:12 before, /device:TPU:32 now
where the time goes in v1:
time: 146 us; the launch traced here: 145 us
  blocking collectives  85.8 us (59%)
  starting transfers between devices  28.3 us (19%)
  waiting for transfers between devices  21.5 us (15%)
  Pallas kernels  6.42 us (4%)
  local copies, waits for them, and re-layouts  1.92 us (1%)
  between operations  1.46 us (1%)
    all_to_all x3, blocking collectives, along_ring(): return lax.all_to_all(x, 'row', 0, 0, axis_index_groups=ring, tiled=True)  52.4 us
    all_to_all x2, blocking collectives, in_plane(): return lax.all_to_all(x, PLANE, 0, 0, tiled=True)  33.4 us
    all_to_all x1, starting transfers between devices, along_ring(): return lax.all_to_all(x, 'row', 0, 0, axis_index_groups=ring, tiled=True)  15.3 us
    all_to_all x1, waiting for transfers between devices, along_ring(): return lax.all_to_all(x, 'row', 0, 0, axis_index_groups=ring, tiled=True)  8.98 us
    all_to_all x1, waiting for transfers between devices, in_plane(): return lax.all_to_all(x, PLANE, 0, 0, tiled=True)  8.86 us
    all_to_all x1, starting transfers between devices, in_plane(): return lax.all_to_all(x, PLANE, 0, 0, tiled=True)  7.04 us
    ppermute x3, starting transfers between devices, swapped(): return lax.ppermute(x, 'row', swap)  5.88 us
    ppermute x3, waiting for transfers between devices, swapped(): return lax.ppermute(x, 'row', swap)  3.64 us
  transfers between devices with their start and end apart: 5, of which 5 were waited for; matrix products, arithmetic and copies ran while one was open for 0% of the time, Pallas kernels for 0%

profile of v1, /device:TPU:32, one launch (start us, length us, event | category | flops | bytes accessed | tf_op | source)
XLA Modules:
  0.0 145.5 jit_solution(12439080088137156627)
XLA Ops:
  0.6 0.0 copy-start.10
  0.6 0.0 copy-start.5
  1.3 0.0 copy-done.10
  1.3 0.1 pad_add_fusion.limit_ref
  1.4 0.0 copy-start.9
  1.4 0.0 copy-done.5
  1.4 0.7 copy-done.9
  2.1 0.0 copy-start.3
  2.1 1.2 copy-done.3
  3.3 1.9 %shard_map.122 = bf16[16,8,1152]{2,1,0:T(8,128)(2,1)} custom-call(s32[2]{0:T(128)S(1)} %pad_add_fusion.limit_ref, s32[1,8]{1,0:T(1,128)S(1)} %copy-done.9, bf16[1,8,1024]{2,1,0:T(8,128)(2,1)S(1)} %copy-done.5, bf16[8,256]{1,0:T(8,128)(2,1)S(1)} %bitcast.25, bf16[1,2,2048,128]{3,2,1,0:T(8,128)(2,1)S(1)} %copy-done.3), custom_call_target="tpu_custom_call" | custom-call | flops 67108864 | bytes 1048576 | tf_op jit(solution)/shard_map/pallas_call | solution.py:236
  5.2 7.0 %all-to-all-start = ((bf16[16,8,1152]{2,1,0:T(8,128)(2,1)}), bf16[16,8,1152]{2,1,0:T(8,128)(2,1)S(1)}, u32[]{:S(2)}, u32[]{:S(2)}) async-start(bf16[16,8,1152]{2,1,0:T(8,128)(2,1)} %shard_map.122), calls=%async_computation | async-start | bytes 589824 | tf_op jit(solution)/shard_map/all_to_all | solution.py:228
  12.3 8.9 %all-to-all-done.in_ref = bf16[16,8,1152]{2,1,0:T(8,128)(2,1)S(1)} async-done(((bf16[16,8,1152]{2,1,0:T(8,128)(2,1)}), bf16[16,8,1152]{2,1,0:T(8,128)(2,1)S(1)}, u32[]{:S(2)}, u32[]{:S(2)}) %all-to-all-start) | async-done | bytes 294944 | tf_op jit(solution)/shard_map/all_to_all | solution.py:228
  21.1 0.0 copy-start.4
  21.1 0.0 copy-start.7
  21.2 0.0 copy-start.2
  21.2 1.3 shard_map.123
  22.5 0.0 copy-start.1
  22.5 15.3 %all-to-all-start.1 = ((bf16[16,8,512]{2,1,0:T(8,128)(2,1)}), bf16[16,8,512]{2,1,0:T(8,128)(2,1)S(1)}, u32[]{:S(2)}, u32[]{:S(2)}) async-start(bf16[16,8,512]{2,1,0:T(8,128)(2,1)} %shard_map.123), calls=%async_computation.1 | async-start | bytes 262144 | tf_op jit(solution)/shard_map/all_to_all | solution.py:225
  37.8 0.0 copy-done.4
  37.8 1.9 %collective-permute-start = (bf16[256,512]{1,0:T(8,128)(2,1)S(1)}, bf16[256,512]{1,0:T(8,128)(2,1)S(1)}, u32[]{:S(2)}, u32[]{:S(2)}) collective-permute-start(bf16[256,512]{1,0:T(8,128)(2,1)S(1)} %copy-done.4), channel_id=1, source_target_pairs={{0,8},{8,0},{16,24},{24,16},{32,40},{40,32},{48,56},{56,48},{64,72... | collective-permute-start | bytes 786440 | tf_op jit(solution)/shard_map/ppermute | solution.py:222
  39.7 1.5 %collective-permute-done.other_ref = bf16[256,512]{1,0:T(8,128)(2,1)S(1)} collective-permute-done((bf16[256,512]{1,0:T(8,128)(2,1)S(1)}, bf16[256,512]{1,0:T(8,128)(2,1)S(1)}, u32[]{:S(2)}, u32[]{:S(2)}) %collective-permute-start) | collective-permute-done | bytes 262176 | tf_op jit(solution)/shard_map/ppermute | solution.py:222
  41.2 9.0 %all-to-all-done.1 = bf16[16,8,512]{2,1,0:T(8,128)(2,1)S(1)} async-done(((bf16[16,8,512]{2,1,0:T(8,128)(2,1)}), bf16[16,8,512]{2,1,0:T(8,128)(2,1)S(1)}, u32[]{:S(2)}, u32[]{:S(2)}) %all-to-all-start.1) | async-done | bytes 131104 | tf_op jit(solution)/shard_map/all_to_all | solution.py:225
  50.2 0.2 shard_map.124
  50.4 17.1 %all_to_all.35.parts_ref = bf16[16,8,512]{2,1,0:T(8,128)(2,1)S(1)} all-to-all(bf16[16,8,512]{2,1,0:T(8,128)(2,1)S(1)} %bitcast.24), channel_id=1, replica_groups={{0,16,32,48,64,80,96,112,128,144,160,176,192,208,224,240},{8,24,40,56,7..., dimensions={0} | all-to-all | bytes 262144 | tf_op jit(solution)/shard_map/all_to_all | solution.py:225
  67.5 0.0 copy-done.7
  67.5 0.6 shard_map.125
  68.2 17.1 %all_to_all.36 = bf16[16,8,512]{2,1,0:T(8,128)(2,1)S(1)} all-to-all(bf16[16,8,512]{2,1,0:T(8,128)(2,1)S(1)} %get-tuple-element.5), channel_id=1, replica_groups={{0,16,32,48,64,80,96,112,128,144,160,176,192,208,224,240},{8,24,40,56,7..., dimensions={0} | all-to-all | bytes 262144 | tf_op jit(solution)/shard_map/all_to_all | solution.py:225
  85.3 0.0 copy-start.6
  85.3 2.0 %collective-permute-start.1 = (bf16[128,512]{1,0:T(8,128)(2,1)S(1)}, bf16[128,512]{1,0:T(8,128)(2,1)S(1)}, u32[]{:S(2)}, u32[]{:S(2)}) collective-permute-start(bf16[128,512]{1,0:T(8,128)(2,1)S(1)} %bitcast.20), channel_id=1, source_target_pairs={{0,8},{8,0},{16,24},{24,16},{32,40},{40,32},{48,56},{56,48},{64,72... | collective-permute-start | bytes 393224 | tf_op jit(solution)/shard_map/ppermute | solution.py:222
  87.3 0.0 copy-done.2
  87.3 0.0 copy-done.1
  87.3 0.0 copy-done.6
  87.3 0.5 shard_map.126.rest_0_
  87.8 0.8 collective-permute-done.1.x_ref
  88.6 0.5 shard_map.127
  89.1 20.2 %all_to_all.37.parts_ref = bf16[16,16,1920]{2,1,0:T(8,128)(2,1)S(1)} all-to-all(bf16[16,16,1920]{2,1,0:T(8,128)(2,1)S(1)} %bitcast.17), channel_id=1, replica_groups=mesh['grp'=2,'row'=32,'col'=8] {'grp','col'}, dimensions={0} | all-to-all | bytes 1966080 | tf_op jit(solution)/shard_map/all_to_all | solution.py:228
  109.3 0.0 copy-start
  109.3 0.2 shard_map.128
  109.5 13.2 %all_to_all.38 = bf16[16,16,896]{2,1,0:T(8,128)(2,1)S(1)} all-to-all(bf16[16,16,896]{2,1,0:T(8,128)(2,1)S(1)} %shard_map.128), channel_id=1, replica_groups=mesh['grp'=2,'row'=32,'col'=8] {'grp','col'}, dimensions={0} | all-to-all | bytes 917504 | tf_op jit(solution)/shard_map/all_to_all | solution.py:228
  122.7 0.0 copy-done
  122.7 0.3 shard_map.129
  123.0 1.9 %collective-permute-start.2 = (bf16[128,512]{1,0:T(8,128)(2,1)S(1)}, bf16[128,512]{1,0:T(8,128)(2,1)S(1)}, u32[]{:S(2)}, u32[]{:S(2)}) collective-permute-start(bf16[128,512]{1,0:T(8,128)(2,1)S(1)} %shard_map.129), channel_id=1, source_target_pairs={{0,8},{8,0},{16,24},{24,16},{32,40},{40,32},{48,56},{56,48},{64,72... | collective-permute-start | bytes 393224 | tf_op jit(solution)/shard_map/ppermute | solution.py:222
  124.9 1.3 collective-permute-done.2.other_ref
  126.2 0.3 shard_map.130
  126.6 0.0 copy-start.8
  126.6 18.3 %all_to_all.39.parts_ref = bf16[16,8,512]{2,1,0:T(8,128)(2,1)S(1)} all-to-all(bf16[16,8,512]{2,1,0:T(8,128)(2,1)S(1)} %bitcast.22), channel_id=1, replica_groups={{0,16,32,48,64,80,96,112,128,144,160,176,192,208,224,240},{8,24,40,56,7..., dimensions={0} | all-to-all | bytes 262144 | tf_op jit(solution)/shard_map/all_to_all | solution.py:225
  144.8 0.0 copy-done.8
  144.8 0.6 shard_map.131
  (1 shorter events, 0.0 us)
Async XLA Ops:
  0.6 0.7 copy-start.10
  0.6 0.8 copy-start.5
  1.4 0.7 copy-start.9
  2.1 1.2 copy-start.3
  5.2 15.9 %all-to-all-start = ((bf16[16,8,1152]{2,1,0:T(8,128)(2,1)}), bf16[16,8,1152]{2,1,0:T(8,128)(2,1)S(1)}, u32[]{:S(2)}, u32[]{:S(2)}) async-start(bf16[16,8,1152]{2,1,0:T(8,128)(2,1)} %shard_map.122), calls=%async_computation | async-start | bytes 589824 | tf_op jit(solution)/shard_map/all_to_all | solution.py:228
  21.1 16.6 %copy-start.4 = (bf16[256,512]{1,0:T(8,128)(2,1)S(1)}, bf16[256,512]{1,0:T(8,128)(2,1)}, u32[]{:S(2)}) copy-start(bf16[256,512]{1,0:T(8,128)(2,1)} %mine_ref.1) | copy-start | bytes 786436
  21.1 46.4 %copy-start.7 = (bf16[8,512]{1,0:T(8,128)(2,1)S(1)}, bf16[8,512]{1,0:T(8,128)(2,1)}, u32[]{:S(2)}) copy-start(bf16[8,512]{1,0:T(8,128)(2,1)} %stream_ref.1) | copy-start | bytes 24580
  21.2 66.2 %copy-start.2 = (bf16[512,896]{1,0:T(8,128)(2,1)S(1)}, bf16[512,896]{1,0:T(8,128)(2,1)}, u32[]{:S(2)}) copy-start(bf16[512,896]{1,0:T(8,128)(2,1)} %up_ref.3) | copy-start | bytes 2752516
  22.5 64.9 %copy-start.1 = (bf16[512,896]{1,0:T(8,128)(2,1)S(1)}, bf16[512,896]{1,0:T(8,128)(2,1)}, u32[]{:S(2)}) copy-start(bf16[512,896]{1,0:T(8,128)(2,1)} %gate_ref.3) | copy-start | bytes 2752516
  22.5 27.8 %all-to-all-start.1 = ((bf16[16,8,512]{2,1,0:T(8,128)(2,1)}), bf16[16,8,512]{2,1,0:T(8,128)(2,1)S(1)}, u32[]{:S(2)}, u32[]{:S(2)}) async-start(bf16[16,8,512]{2,1,0:T(8,128)(2,1)} %shard_map.123), calls=%async_computation.1 | async-start | bytes 262144 | tf_op jit(solution)/shard_map/all_to_all | solution.py:225
  37.8 3.4 %collective-permute-start = (bf16[256,512]{1,0:T(8,128)(2,1)S(1)}, bf16[256,512]{1,0:T(8,128)(2,1)S(1)}, u32[]{:S(2)}, u32[]{:S(2)}) collective-permute-start(bf16[256,512]{1,0:T(8,128)(2,1)S(1)} %copy-done.4), channel_id=1, source_target_pairs={{0,8},{8,0},{16,24},{24,16},{32,40},{40,32},{48,56},{56,48},{64,72... | collective-permute-start | bytes 786440 | tf_op jit(solution)/shard_map/ppermute | solution.py:222
  85.3 2.1 %copy-start.6 = (f32[512]{0:T(512)S(1)}, f32[512]{0:T(512)}, u32[]{:S(2)}) copy-start(f32[512]{0:T(512)} %param.18) | copy-start | bytes 6148
  85.3 3.4 %collective-permute-start.1 = (bf16[128,512]{1,0:T(8,128)(2,1)S(1)}, bf16[128,512]{1,0:T(8,128)(2,1)S(1)}, u32[]{:S(2)}, u32[]{:S(2)}) collective-permute-start(bf16[128,512]{1,0:T(8,128)(2,1)S(1)} %bitcast.20), channel_id=1, source_target_pairs={{0,8},{8,0},{16,24},{24,16},{32,40},{40,32},{48,56},{56,48},{64,72... | collective-permute-start | bytes 393224 | tf_op jit(solution)/shard_map/ppermute | solution.py:222
  109.3 13.4 %copy-start = (bf16[896,512]{1,0:T(8,128)(2,1)S(1)}, bf16[896,512]{1,0:T(8,128)(2,1)}, u32[]{:S(2)}) copy-start(bf16[896,512]{1,0:T(8,128)(2,1)} %weight_ref.3) | copy-start | bytes 2752516
  123.0 3.2 %collective-permute-start.2 = (bf16[128,512]{1,0:T(8,128)(2,1)S(1)}, bf16[128,512]{1,0:T(8,128)(2,1)S(1)}, u32[]{:S(2)}, u32[]{:S(2)}) collective-permute-start(bf16[128,512]{1,0:T(8,128)(2,1)S(1)} %shard_map.129), channel_id=1, source_target_pairs={{0,8},{8,0},{16,24},{24,16},{32,40},{40,32},{48,56},{56,48},{64,72... | collective-permute-start | bytes 393224 | tf_op jit(solution)/shard_map/ppermute | solution.py:222
  126.6 18.3 %copy-start.8 = (bf16[8,512]{1,0:T(8,128)(2,1)S(1)}, bf16[8,512]{1,0:T(8,128)(2,1)}, u32[]{:S(2)}) copy-start(bf16[8,512]{1,0:T(8,128)(2,1)} %get-tuple-element.2.attended_ref) | copy-start | bytes 24580

commit v2 on v1

--- a/solution.py
+++ b/solution.py
@@ -27,7 +27,7 @@
         in_specs=in_specs,
         out_specs=more.pop("out_specs", jax.tree.map(lambda unused: VMEM, out_shape)),
         cost_estimate=pl.CostEstimate(flops=flops, bytes_accessed=moved, transcendentals=0),
-        compiler_params=pltpu.CompilerParams(vmem_limit_bytes=32 * 1024 * 1024),
+        compiler_params=pltpu.CompilerParams(vmem_limit_bytes=16 * 1024 * 1024),
         **more,
     )
 
@@ -91,7 +91,7 @@
         out_ref[k] = line
 
 
-def join_kernel(cols, group, odd_ref, in_ref, out_ref):
+def join_kernel(cols, group, sources, targets, odd_ref, in_ref, out_ref):
     width = group * HD
     odd = odd_ref[0] > 0
     per_block = out_ref.shape[2] // HD
@@ -99,16 +99,15 @@
     for c in range(cols):
         levels = []
         for g in range(2):
-            tail = in_ref[g * cols + c, :, width:].astype(F32)
+            tail = in_ref[sources.index(g * cols + c), :, width:].astype(F32)
             levels.append(
                 tail + jnp.roll(tail, -group, axis=1) + jnp.roll(tail, -2 * group, axis=1)
             )
         share = 1.0 / (1.0 + jnp.exp(levels[1] - levels[0]))
-        rest = 1.0 / (1.0 + jnp.exp(levels[0] - levels[1]))
         for h in range(group):
-            near = in_ref[c, :, h * HD : (h + 1) * HD].astype(F32)
-            far = in_ref[cols + c, :, h * HD : (h + 1) * HD].astype(F32)
-            block.append(near * share[:, h : h + 1] + far * rest[:, h : h + 1])
+            near = in_ref[sources.index(c), :, h * HD : (h + 1) * HD].astype(F32)
+            far = in_ref[sources.index(cols + c), :, h * HD : (h + 1) * HD].astype(F32)
+            block.append(far + (near - far) * share[:, h : h + 1])
             if len(block) == per_block:
                 half = per_block // 2
                 first = jnp.concatenate(block[:half], axis=1)
@@ -116,7 +115,7 @@
                 mine = jnp.where(odd, second, first)
                 other = jnp.where(odd, first, second)
                 number = (c * group + h) // per_block
-                out_ref[number] = jnp.concatenate([mine, other], axis=1).astype(BF)
+                out_ref[targets.index(number)] = jnp.concatenate([mine, other], axis=1).astype(BF)
                 block = []
 
 
@@ -146,20 +145,20 @@
     out_ref[...] = (attended_ref[...].astype(F32) + total(parts_ref)).astype(BF)
 
 
-def widen_kernel(x_ref, gain_ref, gate_ref, up_ref, *rest):
-    out_ref = rest[-1]
-    units = gate_ref.shape[1]
+def widen_kernel(x_ref, gain_ref, *rest):
+    weights, out_ref = rest[:-1], rest[-1]
+    units = weights[0].shape[1]
     x = x_ref[...].astype(F32)
     squares = jnp.sum(x * x, axis=1, keepdims=True)
     scaled = (x * gain_ref[...]).astype(BF)
-    out_ref[:, :units] = jnp.dot(scaled, gate_ref[...], preferred_element_type=F32).astype(BF)
-    out_ref[:, units : 2 * units] = jnp.dot(
-        scaled, up_ref[...], preferred_element_type=F32
-    ).astype(BF)
+    for k, weight_ref in enumerate(weights):
+        out_ref[:, k * units : (k + 1) * units] = jnp.dot(
+            scaled, weight_ref[...], preferred_element_type=F32
+        ).astype(BF)
     high = squares.astype(BF).astype(F32)
     lanes = lax.broadcasted_iota(jnp.int32, (x.shape[0], LANES), 1)
     tail = jnp.where(lanes == 0, high, jnp.where(lanes == 1, squares - high, 0.0))
-    out_ref[:, 2 * units :] = tail.astype(BF)
+    out_ref[:, len(weights) * units :] = tail.astype(BF)
 
 
 def hidden_kernel(units, parts_ref, out_ref):
@@ -179,17 +178,6 @@
         hidden = (gate / (1.0 + jnp.exp(-gate)) * upward).astype(BF)
         for k in range(out_ref.shape[0]):
             out_ref[k, :, start : start + LANES] = hidden
-
-
-def lower_kernel(h_ref, weight_ref, out_ref):
-    out_ref[...] = jnp.dot(h_ref[...], weight_ref[...], preferred_element_type=F32).astype(BF)
-
-
-def lower_add_kernel(h_ref, weight_ref, other_ref, out_ref):
-    out_ref[...] = (
-        jnp.dot(h_ref[...], weight_ref[...], preferred_element_type=F32)
-        + other_ref[...].astype(F32)
-    ).astype(BF)
 
 
 def on_device(
@@ -209,7 +197,10 @@
     cols = lax.axis_size("col")
     plane = lax.axis_size("grp") * cols
     chips = rows // 2
-    ring = [[2 * z + core for z in range(chips)] for core in range(2)]
+    far = chips // 2
+    targets = [(z + far) % chips for z in range(chips)]
+    ring = [[2 * z + core for z in targets] for core in range(2)]
+    sources = [(p + 12) % plane for p in range(plane)]
     swap = [(r, r ^ 1) for r in range(rows)]
     nodes = queries.shape[1]
     group = queries.shape[2] // HD
@@ -225,9 +216,12 @@
         return lax.all_to_all(x, "row", 0, 0, axis_index_groups=ring, tiled=True)
 
     def in_plane(x):
-        return lax.all_to_all(x, PLANE, 0, 0, tiled=True)
+        return lax.all_to_all(x, PLANE, 0, 0, axis_index_groups=[sources], tiled=True)
 
     other_weight = swapped(out_weight)
+    other_gate = swapped(gate_weight)
+    other_up = swapped(up_weight)
+    other_down = swapped(down_weight)
 
     last = lax.axis_index("grp") == lax.axis_size("grp") - 1
     limit = jnp.stack([ctx_len[0] - lax.axis_index("grp") * span, last.astype(jnp.int32)])
@@ -242,7 +236,7 @@
     )(limit.astype(jnp.int32), parents, queries, tree, cache)
     lines = in_plane(lines)
     blocks = call(
-        functools.partial(join_kernel, cols, group),
+        functools.partial(join_kernel, cols, group, sources, targets),
         shape(chips, nodes, D // chips),
         [SMEM, VMEM],
         4 * lines.size,
@@ -267,65 +261,31 @@
     )(parts, stream)
 
     mine = along_ring(copies).reshape(tokens, local)
-    other = swapped(mine)
-    gain = norm_gain.reshape(1, local)
-    wide = 2 * units + LANES
-    flops = 4 * tokens * local * units
-    first = call(
-        widen_kernel,
-        shape(2 * tokens, wide),
-        [VMEM, VMEM, VMEM, VMEM],
-        flops,
-        gate_weight.size * 4,
-        out_specs=pl.BlockSpec((tokens, wide), lambda i: (0, 0)),
-        grid=(1,),
-    )(mine, gain, gate_weight, up_weight)
+    wide = 4 * units + LANES
     expanded = call(
         widen_kernel,
-        shape(2 * tokens, wide),
-        [VMEM, VMEM, VMEM, VMEM, pl.BlockSpec(memory_space=pl.ANY)],
-        flops,
-        gate_weight.size * 4,
-        out_specs=pl.BlockSpec((tokens, wide), lambda i: (1, 0)),
-        grid=(1,),
-        input_output_aliases={4: 0},
-    )(other, gain, gate_weight, up_weight, first)
-    share = 2 * tokens // plane
+        shape(tokens, wide),
+        [VMEM] * 6,
+        8 * tokens * local * units,
+        gate_weight.size * 8,
+    )(mine, norm_gain.reshape(1, local), gate_weight, other_gate, up_weight, other_up)
+    share = tokens // plane
     gathered = in_plane(expanded.reshape(plane, share, wide))
     hidden = call(
-        functools.partial(hidden_kernel, units),
-        shape(plane, share, units),
+        functools.partial(hidden_kernel, 2 * units),
+        shape(plane, share, 2 * units),
         [VMEM],
         gathered.size,
         gathered.size * 2,
     )(gathered)
-    hidden = in_plane(hidden).reshape(2 * tokens, units)
-
-    flops = 2 * tokens * local * units
-    whole = pl.BlockSpec(down_weight.shape, lambda i: (0, 0))
-    theirs = call(
-        lower_kernel,
+    hidden = in_plane(hidden).reshape(tokens, 2 * units)
+    lowered = call(
+        project_kernel,
         shape(tokens, local),
-        [pl.BlockSpec((tokens, units), lambda i: (1, 0)), whole],
-        flops,
-        down_weight.size * 2,
-        grid=(1,),
-        out_specs=pl.BlockSpec((tokens, local), lambda i: (0, 0)),
-    )(hidden, down_weight)
-    received = swapped(theirs)
-    lowered = call(
-        lower_add_kernel,
-        shape(tokens, local),
-        [
-            pl.BlockSpec((tokens, units), lambda i: (0, 0)),
-            whole,
-            pl.BlockSpec((tokens, local), lambda i: (0, 0)),
-        ],
-        flops,
-        down_weight.size * 2,
-        grid=(1,),
-        out_specs=pl.BlockSpec((tokens, local), lambda i: (0, 0)),
-    )(hidden, down_weight, received)
+        [VMEM, VMEM, VMEM],
+        4 * tokens * local * units,
+        down_weight.size * 4,
+    )(hidden, down_weight, other_down)
     parts = along_ring(lowered.reshape(chips, nodes, local))
     layer_output = call(
         final_kernel, shape(nodes, local), [VMEM, VMEM], parts.size, parts.size * 2

time: 146 us -> 135 us (0.925)
  the two profiles are of different devices: /device:TPU:32 before, /device:TPU:16 now
where the time goes in v2:
time: 135 us; the launch traced here: 134 us
  starting transfers between devices  69.8 us (52%)
  waiting for transfers between devices  34.8 us (26%)
  blocking collectives  17.1 us (13%)
  Pallas kernels  9.32 us (7%)
  local copies, waits for them, and re-layouts  1.92 us (1%)
  between operations  1.45 us (1%)
    all_to_all x3, starting transfers between devices, along_ring(): return lax.all_to_all(x, 'row', 0, 0, axis_index_groups=ring, tiled=True)  40 us
    all_to_all x3, waiting for transfers between devices, in_plane(): lax.all_to_all(x, PLANE, 0, 0, axis_index_groups=[sources], tiled=True)  24.5 us
    all_to_all x3, starting transfers between devices, in_plane(): lax.all_to_all(x, PLANE, 0, 0, axis_index_groups=[sources], tiled=True)  21.6 us
    all_to_all x1, blocking collectives, along_ring(): return lax.all_to_all(x, 'row', 0, 0, axis_index_groups=ring, tiled=True)  17.1 us
    all_to_all x3, waiting for transfers between devices, along_ring(): return lax.all_to_all(x, 'row', 0, 0, axis_index_groups=ring, tiled=True)  8.76 us
    ppermute x4, starting transfers between devices, swapped(): return lax.ppermute(x, 'row', swap)  8.17 us
    pallas_call x1, Pallas kernels, on_device(): call(widen_kernel, shape(tokens, wide), [VMEM] * 6, 8 * tokens * local *...  2.86 us
  transfers between devices with their start and end apart: 10, of which 7 were waited for; matrix products, arithmetic and copies ran while one was open for 0% of the time, Pallas kernels for 1%

profile of v2, /device:TPU:16, one launch (start us, length us, event | category | flops | bytes accessed | tf_op | source)
XLA Modules:
  0.0 134.4 jit_solution(553411003648565137)
XLA Ops:
  0.6 0.0 copy-start.10
  0.6 0.0 copy-start.5
  1.3 0.0 copy-done.10
  1.3 0.1 pad_add_fusion.limit_ref
  1.4 0.0 copy-start.9
  1.4 0.0 copy-done.5
  1.4 0.7 copy-done.9
  2.1 0.0 copy-start
  2.1 1.2 copy-done
  3.3 1.9 %shard_map.122 = bf16[16,8,1152]{2,1,0:T(8,128)(2,1)} custom-call(s32[2]{0:T(128)S(1)} %pad_add_fusion.limit_ref, s32[1,8]{1,0:T(1,128)S(1)} %copy-done.9, bf16[1,8,1024]{2,1,0:T(8,128)(2,1)S(1)} %copy-done.5, bf16[8,256]{1,0:T(8,128)(2,1)S(1)} %bitcast.21, bf16[1,2,2048,128]{3,2,1,0:T(8,128)(2,1)S(1)} %copy-done), custom_call_target="tpu_custom_call" | custom-call | flops 67108864 | bytes 1048576 | tf_op jit(solution)/shard_map/pallas_call | solution.py:230
  5.2 0.0 copy-start.4
  5.2 0.0 copy-start.3
  5.2 10.1 %all-to-all-start = ((bf16[16,8,1152]{2,1,0:T(8,128)(2,1)}), bf16[16,8,1152]{2,1,0:T(8,128)(2,1)S(1)}, u32[]{:S(2)}, u32[]{:S(2)}) async-start(bf16[16,8,1152]{2,1,0:T(8,128)(2,1)} %shard_map.122), calls=%async_computation | async-start | bytes 589824 | tf_op jit(solution)/shard_map/all_to_all | solution.py:219
  15.3 0.0 copy-start.2
  15.4 6.3 %all-to-all-done.in_ref = bf16[16,8,1152]{2,1,0:T(8,128)(2,1)S(1)} async-done(((bf16[16,8,1152]{2,1,0:T(8,128)(2,1)}), bf16[16,8,1152]{2,1,0:T(8,128)(2,1)S(1)}, u32[]{:S(2)}, u32[]{:S(2)}) %all-to-all-start) | async-done | bytes 294944 | tf_op jit(solution)/shard_map/all_to_all | solution.py:219
  21.6 0.9 shard_map.123
  22.5 15.8 %all-to-all-start.1 = ((bf16[16,8,512]{2,1,0:T(8,128)(2,1)}), bf16[16,8,512]{2,1,0:T(8,128)(2,1)S(1)}, u32[]{:S(2)}, u32[]{:S(2)}) async-start(bf16[16,8,512]{2,1,0:T(8,128)(2,1)} %shard_map.123), calls=%async_computation.1 | async-start | bytes 262144 | tf_op jit(solution)/shard_map/all_to_all | solution.py:216
  38.3 0.0 copy-done.4
  38.3 1.9 %collective-permute-start = (bf16[256,512]{1,0:T(8,128)(2,1)S(1)}, bf16[256,512]{1,0:T(8,128)(2,1)S(1)}, u32[]{:S(2)}, u32[]{:S(2)}) collective-permute-start(bf16[256,512]{1,0:T(8,128)(2,1)S(1)} %copy-done.4), channel_id=1, source_target_pairs={{0,8},{8,0},{16,24},{24,16},{32,40},{40,32},{48,56},{56,48},{64,72... | collective-permute-start | bytes 786440 | tf_op jit(solution)/shard_map/ppermute | solution.py:213
  40.3 1.5 %collective-permute-done.other_ref = bf16[256,512]{1,0:T(8,128)(2,1)S(1)} collective-permute-done((bf16[256,512]{1,0:T(8,128)(2,1)S(1)}, bf16[256,512]{1,0:T(8,128)(2,1)S(1)}, u32[]{:S(2)}, u32[]{:S(2)}) %collective-permute-start) | collective-permute-done | bytes 262176 | tf_op jit(solution)/shard_map/ppermute | solution.py:213
  41.8 2.1 %all-to-all-done.1 = bf16[16,8,512]{2,1,0:T(8,128)(2,1)S(1)} async-done(((bf16[16,8,512]{2,1,0:T(8,128)(2,1)}), bf16[16,8,512]{2,1,0:T(8,128)(2,1)S(1)}, u32[]{:S(2)}, u32[]{:S(2)}) %all-to-all-start.1) | async-done | bytes 131104 | tf_op jit(solution)/shard_map/all_to_all | solution.py:216
  43.8 0.9 shard_map.124
  44.7 0.0 copy-start.6
  44.7 12.2 %all-to-all-start.2 = ((bf16[16,8,512]{2,1,0:T(8,128)(2,1)}), bf16[16,8,512]{2,1,0:T(8,128)(2,1)S(1)}, u32[]{:S(2)}, u32[]{:S(2)}) async-start(bf16[16,8,512]{2,1,0:T(8,128)(2,1)} %bitcast.5), calls=%async_computation.2 | async-start | bytes 262144 | tf_op jit(solution)/shard_map/all_to_all | solution.py:216
  56.9 0.0 copy-done.2
  56.9 1.9 %collective-permute-start.1 = (bf16[512,896]{1,0:T(8,128)(2,1)S(1)}, bf16[512,896]{1,0:T(8,128)(2,1)S(1)}, u32[]{:S(2)}, u32[]{:S(2)}) collective-permute-start(bf16[512,896]{1,0:T(8,128)(2,1)S(1)} %copy-done.2), channel_id=1, source_target_pairs={{0,8},{8,0},{16,24},{24,16},{32,40},{40,32},{48,56},{56,48},{64,72... | collective-permute-start | bytes 2752520 | tf_op jit(solution)/shard_map/ppermute | solution.py:213
  58.8 0.0 copy-done.3
  58.8 2.4 %collective-permute-start.2 = (bf16[512,896]{1,0:T(8,128)(2,1)S(1)}, bf16[512,896]{1,0:T(8,128)(2,1)}, u32[]{:S(2)}, u32[]{:S(2)}) collective-permute-start(bf16[512,896]{1,0:T(8,128)(2,1)S(1)} %copy-done.3), channel_id=1, source_target_pairs={{0,8},{8,0},{16,24},{24,16},{32,40},{40,32},{48,56},{56,48},{64,72... | collective-permute-start | bytes 2752520 | tf_op jit(solution)/shard_map/ppermute | solution.py:213
  61.3 0.8 all-to-all-done.2.parts_ref
  62.0 0.0 copy-done.6
  62.0 0.7 shard_map.125
  62.7 12.0 %all-to-all-start.3 = ((bf16[16,8,512]{2,1,0:T(8,128)(2,1)}), bf16[16,8,512]{2,1,0:T(8,128)(2,1)S(1)}, u32[]{:S(2)}, u32[]{:S(2)}) async-start(bf16[16,8,512]{2,1,0:T(8,128)(2,1)} %get-tuple-element.5), calls=%async_computation.3 | async-start | bytes 262144 | tf_op jit(solution)/shard_map/all_to_all | solution.py:216
  74.7 0.0 copy-start.8
  74.7 0.0 collective-permute-done.1.rest_1_
  74.7 0.0 collective-permute-done.2.rest_3_
  74.8 5.9 %all-to-all-done.3 = bf16[16,8,512]{2,1,0:T(8,128)(2,1)S(1)} async-done(((bf16[16,8,512]{2,1,0:T(8,128)(2,1)}), bf16[16,8,512]{2,1,0:T(8,128)(2,1)S(1)}, u32[]{:S(2)}, u32[]{:S(2)}) %all-to-all-start.3) | async-done | bytes 131104 | tf_op jit(solution)/shard_map/all_to_all | solution.py:216
  80.7 0.0 copy-done.8
  80.7 2.9 %shard_map.126 = bf16[128,3712]{1,0:T(8,128)(2,1)} custom-call(bf16[128,512]{1,0:T(8,128)(2,1)S(1)} %bitcast.18, f32[1,512]{1,0:T(1,128)S(1)} %bitcast.22, bf16[512,896]{1,0:T(8,128)(2,1)S(1)} %copy-done.2, bf16[512,896]{1,0:T(8,128)(2,1)S(1)} %collective-permute-done.1.rest_1_, bf16[512,896]{1,0:T(8,128)(2,1)S(1)} %copy-done.3, ...), custom_call_target="tpu_custom_call" | custom-call | flops 469762048 | bytes 3670016 | tf_op jit(solution)/shard_map/pallas_call | solution.py:265
  83.5 0.0 copy-start.1
  83.5 6.2 %all-to-all-start.4 = ((bf16[16,8,3712]{2,1,0:T(8,128)(2,1)}), bf16[16,8,3712]{2,1,0:T(8,128)(2,1)S(1)}, u32[]{:S(2)}, u32[]{:S(2)}) async-start(bf16[16,8,3712]{2,1,0:T(8,128)(2,1)} %bitcast.8), calls=%async_computation.4 | async-start | bytes 1900544 | tf_op jit(solution)/shard_map/all_to_all | solution.py:219
  89.7 0.0 copy-done.1
  89.7 1.9 %collective-permute-start.3 = (bf16[896,512]{1,0:T(8,128)(2,1)S(1)}, bf16[896,512]{1,0:T(8,128)(2,1)S(1)}, u32[]{:S(2)}, u32[]{:S(2)}) collective-permute-start(bf16[896,512]{1,0:T(8,128)(2,1)S(1)} %copy-done.1), channel_id=1, source_target_pairs={{0,8},{8,0},{16,24},{24,16},{32,40},{40,32},{48,56},{56,48},{64,72... | collective-permute-start | bytes 2752520 | tf_op jit(solution)/shard_map/ppermute | solution.py:213
  91.7 10.8 %all-to-all-done.4.parts_ref = bf16[16,8,3712]{2,1,0:T(8,128)(2,1)S(1)} async-done(((bf16[16,8,3712]{2,1,0:T(8,128)(2,1)}), bf16[16,8,3712]{2,1,0:T(8,128)(2,1)S(1)}, u32[]{:S(2)}, u32[]{:S(2)}) %all-to-all-start.4) | async-done | bytes 950304 | tf_op jit(solution)/shard_map/all_to_all | solution.py:219
  102.5 1.0 shard_map.127
  103.5 5.3 %all-to-all-start.5 = ((bf16[16,8,1792]{2,1,0:T(8,128)(2,1)}), bf16[16,8,1792]{2,1,0:T(8,128)(2,1)S(1)}, u32[]{:S(2)}, u32[]{:S(2)}) async-start(bf16[16,8,1792]{2,1,0:T(8,128)(2,1)} %shard_map.127), calls=%async_computation.5 | async-start | bytes 917504 | tf_op jit(solution)/shard_map/all_to_all | solution.py:219
  108.8 0.0 collective-permute-done.3.other_ref
  108.8 7.5 %all-to-all-done.5 = bf16[16,8,1792]{2,1,0:T(8,128)(2,1)S(1)} async-done(((bf16[16,8,1792]{2,1,0:T(8,128)(2,1)}), bf16[16,8,1792]{2,1,0:T(8,128)(2,1)S(1)}, u32[]{:S(2)}, u32[]{:S(2)}) %all-to-all-start.5) | async-done | bytes 458784 | tf_op jit(solution)/shard_map/all_to_all | solution.py:219
  116.2 0.4 shard_map.128
  116.7 0.0 copy-start.7
  116.7 17.1 %all_to_all.35.parts_ref = bf16[16,8,512]{2,1,0:T(8,128)(2,1)S(1)} all-to-all(bf16[16,8,512]{2,1,0:T(8,128)(2,1)S(1)} %bitcast.19), channel_id=1, replica_groups={{128,144,160,176,192,208,224,240,0,16,32,48,64,80,96,112},{136,152,168,..., dimensions={0} | all-to-all | bytes 262144 | tf_op jit(solution)/shard_map/all_to_all | solution.py:216
  133.8 0.0 copy-done.7
  133.8 0.6 shard_map.129
  (1 shorter events, 0.0 us)
Async XLA Ops:
  0.6 0.7 copy-start.10
  0.6 0.8 copy-start.5
  1.4 0.7 copy-start.9
  2.1 1.2 copy-start
  5.2 33.1 %copy-start.4 = (bf16[256,512]{1,0:T(8,128)(2,1)S(1)}, bf16[256,512]{1,0:T(8,128)(2,1)}, u32[]{:S(2)}) copy-start(bf16[256,512]{1,0:T(8,128)(2,1)} %mine_ref.2) | copy-start | bytes 786436
  5.2 53.6 %copy-start.3 = (bf16[512,896]{1,0:T(8,128)(2,1)S(1)}, bf16[512,896]{1,0:T(8,128)(2,1)}, u32[]{:S(2)}) copy-start(bf16[512,896]{1,0:T(8,128)(2,1)} %rest_2_.1) | copy-start | bytes 2752516
  5.2 16.4 %all-to-all-start = ((bf16[16,8,1152]{2,1,0:T(8,128)(2,1)}), bf16[16,8,1152]{2,1,0:T(8,128)(2,1)S(1)}, u32[]{:S(2)}, u32[]{:S(2)}) async-start(bf16[16,8,1152]{2,1,0:T(8,128)(2,1)} %shard_map.122), calls=%async_computation | async-start | bytes 589824 | tf_op jit(solution)/shard_map/all_to_all | solution.py:219
  15.3 41.6 %copy-start.2 = (bf16[512,896]{1,0:T(8,128)(2,1)S(1)}, bf16[512,896]{1,0:T(8,128)(2,1)}, u32[]{:S(2)}) copy-start(bf16[512,896]{1,0:T(8,128)(2,1)} %rest_0_.1) | copy-start | bytes 2752516
  22.5 21.3 %all-to-all-start.1 = ((bf16[16,8,512]{2,1,0:T(8,128)(2,1)}), bf16[16,8,512]{2,1,0:T(8,128)(2,1)S(1)}, u32[]{:S(2)}, u32[]{:S(2)}) async-start(bf16[16,8,512]{2,1,0:T(8,128)(2,1)} %shard_map.123), calls=%async_computation.1 | async-start | bytes 262144 | tf_op jit(solution)/shard_map/all_to_all | solution.py:216
  38.3 3.4 %collective-permute-start = (bf16[256,512]{1,0:T(8,128)(2,1)S(1)}, bf16[256,512]{1,0:T(8,128)(2,1)S(1)}, u32[]{:S(2)}, u32[]{:S(2)}) collective-permute-start(bf16[256,512]{1,0:T(8,128)(2,1)S(1)} %copy-done.4), channel_id=1, source_target_pairs={{0,8},{8,0},{16,24},{24,16},{32,40},{40,32},{48,56},{56,48},{64,72... | collective-permute-start | bytes 786440 | tf_op jit(solution)/shard_map/ppermute | solution.py:213
  44.7 17.3 %copy-start.6 = (bf16[8,512]{1,0:T(8,128)(2,1)S(1)}, bf16[8,512]{1,0:T(8,128)(2,1)}, u32[]{:S(2)}) copy-start(bf16[8,512]{1,0:T(8,128)(2,1)} %stream_ref.1) | copy-start | bytes 24580
  44.7 17.3 %all-to-all-start.2 = ((bf16[16,8,512]{2,1,0:T(8,128)(2,1)}), bf16[16,8,512]{2,1,0:T(8,128)(2,1)S(1)}, u32[]{:S(2)}, u32[]{:S(2)}) async-start(bf16[16,8,512]{2,1,0:T(8,128)(2,1)} %bitcast.5), calls=%async_computation.2 | async-start | bytes 262144 | tf_op jit(solution)/shard_map/all_to_all | solution.py:216
  56.9 17.8 %collective-permute-start.1 = (bf16[512,896]{1,0:T(8,128)(2,1)S(1)}, bf16[512,896]{1,0:T(8,128)(2,1)S(1)}, u32[]{:S(2)}, u32[]{:S(2)}) collective-permute-start(bf16[512,896]{1,0:T(8,128)(2,1)S(1)} %copy-done.2), channel_id=1, source_target_pairs={{0,8},{8,0},{16,24},{24,16},{32,40},{40,32},{48,56},{56,48},{64,72... | collective-permute-start | bytes 2752520 | tf_op jit(solution)/shard_map/ppermute | solution.py:213
  58.8 15.9 %collective-permute-start.2 = (bf16[512,896]{1,0:T(8,128)(2,1)S(1)}, bf16[512,896]{1,0:T(8,128)(2,1)}, u32[]{:S(2)}, u32[]{:S(2)}) collective-permute-start(bf16[512,896]{1,0:T(8,128)(2,1)S(1)} %copy-done.3), channel_id=1, source_target_pairs={{0,8},{8,0},{16,24},{24,16},{32,40},{40,32},{48,56},{56,48},{64,72... | collective-permute-start | bytes 2752520 | tf_op jit(solution)/shard_map/ppermute | solution.py:213
  62.7 18.0 %all-to-all-start.3 = ((bf16[16,8,512]{2,1,0:T(8,128)(2,1)}), bf16[16,8,512]{2,1,0:T(8,128)(2,1)S(1)}, u32[]{:S(2)}, u32[]{:S(2)}) async-start(bf16[16,8,512]{2,1,0:T(8,128)(2,1)} %get-tuple-element.5), calls=%async_computation.3 | async-start | bytes 262144 | tf_op jit(solution)/shard_map/all_to_all | solution.py:216
  74.7 6.0 %copy-start.8 = (f32[512]{0:T(512)S(1)}, f32[512]{0:T(512)}, u32[]{:S(2)}) copy-start(f32[512]{0:T(512)} %param.18) | copy-start | bytes 6148
  83.5 6.2 %copy-start.1 = (bf16[896,512]{1,0:T(8,128)(2,1)S(1)}, bf16[896,512]{1,0:T(8,128)(2,1)}, u32[]{:S(2)}) copy-start(bf16[896,512]{1,0:T(8,128)(2,1)} %mine_ref.3) | copy-start | bytes 2752516
  83.5 18.9 %all-to-all-start.4 = ((bf16[16,8,3712]{2,1,0:T(8,128)(2,1)}), bf16[16,8,3712]{2,1,0:T(8,128)(2,1)S(1)}, u32[]{:S(2)}, u32[]{:S(2)}) async-start(bf16[16,8,3712]{2,1,0:T(8,128)(2,1)} %bitcast.8), calls=%async_computation.4 | async-start | bytes 1900544 | tf_op jit(solution)/shard_map/all_to_all | solution.py:219
  89.7 19.0 %collective-permute-start.3 = (bf16[896,512]{1,0:T(8,128)(2,1)S(1)}, bf16[896,512]{1,0:T(8,128)(2,1)S(1)}, u32[]{:S(2)}, u32[]{:S(2)}) collective-permute-start(bf16[896,512]{1,0:T(8,128)(2,1)S(1)} %copy-done.1), channel_id=1, source_target_pairs={{0,8},{8,0},{16,24},{24,16},{32,40},{40,32},{48,56},{56,48},{64,72... | collective-permute-start | bytes 2752520 | tf_op jit(solution)/shard_map/ppermute | solution.py:213
  103.5 12.8 %all-to-all-start.5 = ((bf16[16,8,1792]{2,1,0:T(8,128)(2,1)}), bf16[16,8,1792]{2,1,0:T(8,128)(2,1)S(1)}, u32[]{:S(2)}, u32[]{:S(2)}) async-start(bf16[16,8,1792]{2,1,0:T(8,128)(2,1)} %shard_map.127), calls=%async_computation.5 | async-start | bytes 917504 | tf_op jit(solution)/shard_map/all_to_all | solution.py:219
  116.7 17.1 %copy-start.7 = (bf16[8,512]{1,0:T(8,128)(2,1)S(1)}, bf16[8,512]{1,0:T(8,128)(2,1)}, u32[]{:S(2)}) copy-start(bf16[8,512]{1,0:T(8,128)(2,1)} %get-tuple-element.2.attended_ref) | copy-start | bytes 24580

commit v3 on v2

--- a/solution.py
+++ b/solution.py
@@ -16,6 +16,8 @@
 LANES = 128
 VMEM = pl.BlockSpec(memory_space=pltpu.VMEM)
 SMEM = pl.BlockSpec(memory_space=pltpu.SMEM)
+ANY = pl.BlockSpec(memory_space=pl.ANY)
+HBM = pl.BlockSpec(memory_space=pltpu.HBM)
 BF = jnp.bfloat16
 F32 = jnp.float32
 
@@ -27,7 +29,7 @@
         in_specs=in_specs,
         out_specs=more.pop("out_specs", jax.tree.map(lambda unused: VMEM, out_shape)),
         cost_estimate=pl.CostEstimate(flops=flops, bytes_accessed=moved, transcendentals=0),
-        compiler_params=pltpu.CompilerParams(vmem_limit_bytes=16 * 1024 * 1024),
+        compiler_params=pltpu.CompilerParams(vmem_limit_bytes=more.pop("vmem", 16) * 1024 * 1024),
         **more,
     )
 
@@ -36,16 +38,54 @@
     return jax.ShapeDtypeStruct(dims, kind)
 
 
-def attend_kernel(copies, nodes, group, limit_ref, parents_ref, q_ref, tree_ref, cache_ref, out_ref):
+def attend_kernel(
+    nodes,
+    group,
+    pieces,
+    length_ref,
+    parents_ref,
+    q_ref,
+    tree_ref,
+    cache_ref,
+    out_ref,
+    length,
+    parents,
+    q_wide,
+    tree_pair,
+    cached,
+    sems,
+    cache_sems,
+):
     span = cache_ref.shape[2]
     rows = nodes * group
     scale = 1.0 / math.sqrt(HD)
-    wide = q_ref[0].astype(F32)
+    small = [
+        pltpu.make_async_copy(source, target, sems.at[k])
+        for k, (source, target) in enumerate(
+            [(q_ref, q_wide), (length_ref, length), (parents_ref, parents), (tree_ref, tree_pair)]
+        )
+    ]
+    size = span // pieces
+    large = [
+        pltpu.make_async_copy(
+            cache_ref.at[0, part, pl.ds(k * size, size)],
+            cached.at[part, pl.ds(k * size, size)],
+            cache_sems.at[part, k],
+        )
+        for part in range(2)
+        for k in range(pieces)
+    ]
+    for copy in small + large:
+        copy.start()
+    for copy in small:
+        copy.wait()
+    place = lax.axis_index("grp")
+    limit = length[0, 0] - place * span
+    tree_here = (place == lax.axis_size("grp") - 1).astype(jnp.int32)
+
+    wide = q_wide[0].astype(F32)
     q = jnp.concatenate([wide[:, h * HD : (h + 1) * HD] for h in range(group)], axis=0).astype(BF)
     contract = (((1,), (1,)), ((), ()))
-    scores = lax.dot_general(q, cache_ref[0, 0], contract, preferred_element_type=F32) * scale
-    position = lax.broadcasted_iota(jnp.int32, (rows, span), 1)
-    scores = jnp.where(position < limit_ref[0], scores, FLOOR)
 
     lane = lax.broadcasted_iota(jnp.int32, (nodes, nodes), 1)
     here = lax.broadcasted_iota(jnp.int32, (nodes, nodes), 0)
@@ -54,25 +94,33 @@
         reach = jnp.where(lane == here, 1, reach)
         above = jnp.full((nodes, nodes), -1, jnp.int32)
         for j in range(nodes):
-            above = jnp.where(here == j, parents_ref[0, j], above)
+            above = jnp.where(here == j, parents[0, j], above)
         here = above
-    reach = reach * limit_ref[1]
-    reach = jnp.concatenate([reach] * group, axis=0)
-    tree_keys = tree_ref[:, :HD]
-    tree_values = tree_ref[:, HD:].astype(F32)
+    reach = jnp.concatenate([reach * tree_here] * group, axis=0)
+    pair = tree_pair[0].astype(F32)
+    tree_keys = pair[:, 0, :].astype(BF)
+    tree_values = pair[:, 1, :]
     tree_scores = lax.dot_general(q, tree_keys, contract, preferred_element_type=F32) * scale
     tree_scores = jnp.where(reach > 0, tree_scores, FLOOR)
-
-    maxima = jnp.maximum(
-        jnp.max(scores, axis=1, keepdims=True), jnp.max(tree_scores, axis=1, keepdims=True)
-    )
-    weights = jnp.exp(scores - maxima)
+    maxima = jnp.max(tree_scores, axis=1, keepdims=True)
+
+    for copy in large[:pieces]:
+        copy.wait()
+    scores = lax.dot_general(q, cached[0], contract, preferred_element_type=F32) * scale
+    position = lax.broadcasted_iota(jnp.int32, (rows, span), 1)
+    scores = jnp.where(position < limit, scores, FLOOR)
+    maxima = jnp.maximum(maxima, jnp.max(scores, axis=1, keepdims=True))
     tree_weights = jnp.exp(tree_scores - maxima)
-    totals = jnp.sum(weights, axis=1, keepdims=True) + jnp.sum(tree_weights, axis=1, keepdims=True)
-    summed = jnp.dot(weights.astype(BF), cache_ref[0, 1], preferred_element_type=F32)
+    totals = jnp.sum(tree_weights, axis=1, keepdims=True)
     tree_rounded = tree_weights.astype(BF).astype(F32)
+    summed = jnp.zeros((rows, HD), F32)
     for j in range(nodes):
         summed = summed + tree_rounded[:, j : j + 1] * tree_values[j : j + 1, :]
+    weights = jnp.exp(scores - maxima)
+    totals = totals + jnp.sum(weights, axis=1, keepdims=True)
+    for copy in large[pieces:]:
+        copy.wait()
+    summed = summed + jnp.dot(weights.astype(BF), cached[1], preferred_element_type=F32)
     heads = summed / totals
     level = maxima + jnp.log(totals)
 
@@ -87,7 +135,7 @@
     line = jnp.concatenate(
         [heads[h * nodes : (h + 1) * nodes] for h in range(group)] + [tail], axis=1
     ).astype(BF)
-    for k in range(copies):
+    for k in range(out_ref.shape[0]):
         out_ref[k] = line
 
 
@@ -146,19 +194,38 @@
 
 
 def widen_kernel(x_ref, gain_ref, *rest):
-    weights, out_ref = rest[:-1], rest[-1]
+    weights, (out_ref, held, sems) = rest[:4], rest[4:]
     units = weights[0].shape[1]
+    size = held.shape[1] // sems.shape[1]
+    arriving = [
+        [
+            pltpu.make_async_copy(
+                weights[k + 1].at[pl.ds(j * size, size)],
+                held.at[k, pl.ds(j * size, size)],
+                sems.at[k, j],
+            )
+            for j in range(sems.shape[1])
+        ]
+        for k in range(held.shape[0])
+    ]
+    for copies in arriving:
+        for copy in copies:
+            copy.start()
     x = x_ref[...].astype(F32)
+    scaled = (x * gain_ref[...]).astype(BF)
     squares = jnp.sum(x * x, axis=1, keepdims=True)
-    scaled = (x * gain_ref[...]).astype(BF)
-    for k, weight_ref in enumerate(weights):
-        out_ref[:, k * units : (k + 1) * units] = jnp.dot(
-            scaled, weight_ref[...], preferred_element_type=F32
-        ).astype(BF)
     high = squares.astype(BF).astype(F32)
     lanes = lax.broadcasted_iota(jnp.int32, (x.shape[0], LANES), 1)
     tail = jnp.where(lanes == 0, high, jnp.where(lanes == 1, squares - high, 0.0))
-    out_ref[:, len(weights) * units :] = tail.astype(BF)
+    out_ref[:, 4 * units :] = tail.astype(BF)
+    for k in range(4):
+        if k > 0:
+            for copy in arriving[k - 1]:
+                copy.wait()
+        weight = weights[0][...] if k == 0 else held[k - 1]
+        out_ref[:, k * units : (k + 1) * units] = jnp.dot(
+            scaled, weight, preferred_element_type=F32
+        ).astype(BF)
 
 
 def hidden_kernel(units, parts_ref, out_ref):
@@ -223,18 +290,26 @@
     other_up = swapped(up_weight)
     other_down = swapped(down_weight)
 
-    last = lax.axis_index("grp") == lax.axis_size("grp") - 1
-    limit = jnp.stack([ctx_len[0] - lax.axis_index("grp") * span, last.astype(jnp.int32)])
-    tree = tree_kv.reshape(nodes, 2 * HD)
     width = group * HD
+    pieces = 2
     lines = call(
-        functools.partial(attend_kernel, plane, nodes, group),
+        functools.partial(attend_kernel, nodes, group, pieces),
         shape(plane, nodes, width + LANES),
-        [SMEM, SMEM, VMEM, VMEM, VMEM],
+        [ANY] * 5,
         4 * nodes * group * span * HD,
         cache.size * 2,
-    )(limit.astype(jnp.int32), parents, queries, tree, cache)
-    lines = in_plane(lines)
+        scratch_shapes=[
+            pltpu.SMEM((1, 1), jnp.int32),
+            pltpu.SMEM(parents.shape, jnp.int32),
+            pltpu.VMEM(queries.shape, BF),
+            pltpu.VMEM(tree_kv.shape, BF),
+            pltpu.VMEM(cache.shape[1:], BF),
+            pltpu.SemaphoreType.DMA((4,)),
+            pltpu.SemaphoreType.DMA((2, pieces)),
+        ],
+        vmem=56,
+    )(ctx_len.reshape(1, 1), parents, queries, tree_kv, cache)
+    lines, other_weight = lax.optimization_barrier((in_plane(lines), other_weight))
     blocks = call(
         functools.partial(join_kernel, cols, group, sources, targets),
         shape(chips, nodes, D // chips),
@@ -251,7 +326,9 @@
         2 * tokens * local * (D // chips),
         out_weight.size * 4,
     )(portion, out_weight, other_weight)
-    parts = along_ring(partial.reshape(chips, nodes, local))
+    parts, other_gate, other_up = lax.optimization_barrier(
+        (along_ring(partial.reshape(chips, nodes, local)), other_gate, other_up)
+    )
     attended, copies = call(
         residual_kernel,
         (shape(nodes, local), shape(chips, nodes, local)),
@@ -260,14 +337,19 @@
         parts.size * 4,
     )(parts, stream)
 
-    mine = along_ring(copies).reshape(tokens, local)
+    mine, other_down = lax.optimization_barrier((along_ring(copies), other_down))
+    mine = mine.reshape(tokens, local)
     wide = 4 * units + LANES
     expanded = call(
         widen_kernel,
         shape(tokens, wide),
-        [VMEM] * 6,
+        [VMEM] * 3 + [HBM] * 3,
         8 * tokens * local * units,
         gate_weight.size * 8,
+        scratch_shapes=[
+            pltpu.VMEM((3,) + up_weight.shape, BF),
+            pltpu.SemaphoreType.DMA((3, 2)),
+        ],
     )(mine, norm_gain.reshape(1, local), gate_weight, other_gate, up_weight, other_up)
     share = tokens // plane
     gathered = in_plane(expanded.reshape(plane, share, wide))

time: 135 us -> 130 us (0.963)
  blocking collectives: 17.1 us -> 46.9 us
  waiting for transfers between devices: 34.8 us -> 14 us
  starting transfers between devices: 69.8 us -> 58.4 us
  local copies, waits for them, and re-layouts: 1.92 us -> 0.03 us
    all_to_all x0 -> x2, blocking collectives: none -> 29.9 us  [in_plane(): lax.all_to_all(x, PLANE, 0, 0, axis_index_groups=[sources], tiled=True)]
    all_to_all x3 -> x1, waiting for transfers between devices: 24.5 us -> 2.71 us  [in_plane(): lax.all_to_all(x, PLANE, 0, 0, axis_index_groups=[sources], tiled=True)]
    all_to_all x3 -> x1, starting transfers between devices: 21.6 us -> 10.1 us  [in_plane(): lax.all_to_all(x, PLANE, 0, 0, axis_index_groups=[sources], tiled=True)]
    unnamed x23 -> x12, local copies, waits for them, and re-layouts: 1.92 us -> 0.03 us
  transfers between devices with their start and end apart: 10 -> 8, of which waited for: 7 -> 5; matrix products, arithmetic and copies ran while one was open for 0% -> 0% of each run, Pallas kernels for 1% -> 1%
where the time goes in v3:
time: 130 us
  starting transfers between devices  58.4 us (45%)
  blocking collectives  46.9 us (36%)
  waiting for transfers between devices  14 us (11%)
  Pallas kernels  8.8 us (7%)
  between operations  1.43 us (1%)
    all_to_all x3, starting transfers between devices, along_ring(): return lax.all_to_all(x, 'row', 0, 0, axis_index_groups=ring, tiled=True)  40 us
    all_to_all x2, blocking collectives, in_plane(): lax.all_to_all(x, PLANE, 0, 0, axis_index_groups=[sources], tiled=True)  29.9 us
    all_to_all x1, blocking collectives, along_ring(): return lax.all_to_all(x, 'row', 0, 0, axis_index_groups=ring, tiled=True)  17 us
    all_to_all x1, starting transfers between devices, in_plane(): lax.all_to_all(x, PLANE, 0, 0, axis_index_groups=[sources], tiled=True)  10.1 us
    all_to_all x3, waiting for transfers between devices, along_ring(): return lax.all_to_all(x, 'row', 0, 0, axis_index_groups=ring, tiled=True)  9.84 us
    ppermute x4, starting transfers between devices, swapped(): return lax.ppermute(x, 'row', swap)  8.3 us
    pallas_call x1, Pallas kernels, on_device(): call(functools.partial(attend_kernel, nodes, group, pieces), shape(plane,...  2.85 us
    all_to_all x1, waiting for transfers between devices, in_plane(): lax.all_to_all(x, PLANE, 0, 0, axis_index_groups=[sources], tiled=True)  2.71 us
  transfers between devices with their start and end apart: 8, of which 5 were waited for; matrix products, arithmetic and copies ran while one was open for 0% of the time, Pallas kernels for 1%

profile of v3, /device:TPU:16, one launch (start us, length us, event | category | flops | bytes accessed | tf_op | source)
XLA Modules:
  0.0 129.6 jit_solution(9310448764838899200)
XLA Ops:
  1.3 0.0 copy-start.2
  1.3 2.8 %shard_map.122 = bf16[16,8,1152]{2,1,0:T(8,128)(2,1)} custom-call(s32[1,1]{1,0:T(1,128)} %bitcast.9.length_ref, s32[1,8]{1,0:T(1,128)} %parents_ref.1, bf16[1,8,1024]{2,1,0:T(8,128)(2,1)} %q_ref.1, bf16[1,8,2,128]{3,2,1,0:T(2,128)(2,1)} %tree_ref.1, bf16[1,2,2048,128]{3,2,1,0:T(8,128)(2,1)} %cache_ref.1), custom_call_target="tpu_custom_call" | custom-call | flops 67108864 | bytes 1048576 | tf_op jit(solution)/shard_map/pallas_call | solution.py:295
  4.1 0.0 copy-start.1
  4.2 10.1 %all-to-all-start = ((bf16[16,8,1152]{2,1,0:T(8,128)(2,1)}), bf16[16,8,1152]{2,1,0:T(8,128)(2,1)S(1)}, u32[]{:S(2)}, u32[]{:S(2)}) async-start(bf16[16,8,1152]{2,1,0:T(8,128)(2,1)} %shard_map.122), calls=%async_computation | async-start | bytes 589824 | tf_op jit(solution)/shard_map/all_to_all | solution.py:286
  14.3 0.0 copy-done.2
  14.3 0.0 copy-start
  14.3 2.1 %collective-permute-start = (bf16[256,512]{1,0:T(8,128)(2,1)S(1)}, bf16[256,512]{1,0:T(8,128)(2,1)S(1)}, u32[]{:S(2)}, u32[]{:S(2)}) collective-permute-start(bf16[256,512]{1,0:T(8,128)(2,1)S(1)} %copy-done.2), channel_id=1, source_target_pairs={{0,8},{8,0},{16,24},{24,16},{32,40},{40,32},{48,56},{56,48},{64,72... | collective-permute-start | bytes 786440 | tf_op jit(solution)/shard_map/ppermute | solution.py:280
  16.4 1.5 %collective-permute-done.other_ref = bf16[256,512]{1,0:T(8,128)(2,1)S(1)} collective-permute-done((bf16[256,512]{1,0:T(8,128)(2,1)S(1)}, bf16[256,512]{1,0:T(8,128)(2,1)S(1)}, u32[]{:S(2)}, u32[]{:S(2)}) %collective-permute-start) | collective-permute-done | bytes 262176 | tf_op jit(solution)/shard_map/ppermute | solution.py:280
  17.9 2.7 %all-to-all-done.in_ref = bf16[16,8,1152]{2,1,0:T(8,128)(2,1)S(1)} async-done(((bf16[16,8,1152]{2,1,0:T(8,128)(2,1)}), bf16[16,8,1152]{2,1,0:T(8,128)(2,1)S(1)}, u32[]{:S(2)}, u32[]{:S(2)}) %all-to-all-start) | async-done | bytes 294944 | tf_op jit(solution)/shard_map/all_to_all | solution.py:286
  20.6 0.9 shard_map.123
  21.5 15.8 %all-to-all-start.1 = ((bf16[16,8,512]{2,1,0:T(8,128)(2,1)}), bf16[16,8,512]{2,1,0:T(8,128)(2,1)S(1)}, u32[]{:S(2)}, u32[]{:S(2)}) async-start(bf16[16,8,512]{2,1,0:T(8,128)(2,1)} %shard_map.123), calls=%async_computation.1 | async-start | bytes 262144 | tf_op jit(solution)/shard_map/all_to_all | solution.py:283
  37.3 0.0 copy-done.1
  37.3 1.9 %collective-permute-start.1 = (bf16[512,896]{1,0:T(8,128)(2,1)S(1)}, bf16[512,896]{1,0:T(8,128)(2,1)}, u32[]{:S(2)}, u32[]{:S(2)}) collective-permute-start(bf16[512,896]{1,0:T(8,128)(2,1)S(1)} %copy-done.1), channel_id=1, source_target_pairs={{0,8},{8,0},{16,24},{24,16},{32,40},{40,32},{48,56},{56,48},{64,72... | collective-permute-start | bytes 2752520 | tf_op jit(solution)/shard_map/ppermute | solution.py:280
  39.2 2.4 %collective-permute-start.2 = (bf16[512,896]{1,0:T(8,128)(2,1)}, bf16[512,896]{1,0:T(8,128)(2,1)}, u32[]{:S(2)}, u32[]{:S(2)}) collective-permute-start(bf16[512,896]{1,0:T(8,128)(2,1)} %rest_2_.1), channel_id=1, source_target_pairs={{0,8},{8,0},{16,24},{24,16},{32,40},{40,32},{48,56},{56,48},{64,72... | collective-permute-start | bytes 2752520 | tf_op jit(solution)/shard_map/ppermute | solution.py:280
  41.6 1.2 all-to-all-done.1
  42.8 0.9 shard_map.124
  43.7 0.0 copy-start.3
  43.7 12.2 %all-to-all-start.2 = ((bf16[16,8,512]{2,1,0:T(8,128)(2,1)}), bf16[16,8,512]{2,1,0:T(8,128)(2,1)S(1)}, u32[]{:S(2)}, u32[]{:S(2)}) async-start(bf16[16,8,512]{2,1,0:T(8,128)(2,1)} %bitcast.3), calls=%async_computation.2 | async-start | bytes 262144 | tf_op jit(solution)/shard_map/all_to_all | solution.py:283
  55.9 0.0 copy-done
  55.9 1.9 %collective-permute-start.3 = (bf16[896,512]{1,0:T(8,128)(2,1)S(1)}, bf16[896,512]{1,0:T(8,128)(2,1)S(1)}, u32[]{:S(2)}, u32[]{:S(2)}) collective-permute-start(bf16[896,512]{1,0:T(8,128)(2,1)S(1)} %copy-done), channel_id=1, source_target_pairs={{0,8},{8,0},{16,24},{24,16},{32,40},{40,32},{48,56},{56,48},{64,72... | collective-permute-start | bytes 2752520 | tf_op jit(solution)/shard_map/ppermute | solution.py:280
  57.8 0.0 collective-permute-done.1.rest_1_
  57.8 0.0 collective-permute-done.2.rest_3_
  57.8 3.6 %all-to-all-done.2.parts_ref = bf16[16,8,512]{2,1,0:T(8,128)(2,1)S(1)} async-done(((bf16[16,8,512]{2,1,0:T(8,128)(2,1)}), bf16[16,8,512]{2,1,0:T(8,128)(2,1)S(1)}, u32[]{:S(2)}, u32[]{:S(2)}) %all-to-all-start.2) | async-done | bytes 131104 | tf_op jit(solution)/shard_map/all_to_all | solution.py:283
  61.4 0.0 copy-done.3
  61.4 0.7 shard_map.125
  62.1 12.0 %all-to-all-start.3 = ((bf16[16,8,512]{2,1,0:T(8,128)(2,1)}), bf16[16,8,512]{2,1,0:T(8,128)(2,1)S(1)}, u32[]{:S(2)}, u32[]{:S(2)}) async-start(bf16[16,8,512]{2,1,0:T(8,128)(2,1)} %get-tuple-element.15), calls=%async_computation.3 | async-start | bytes 262144 | tf_op jit(solution)/shard_map/all_to_all | solution.py:283
  74.1 0.0 copy-start.5
  74.1 0.0 collective-permute-done.3.other_ref
  74.1 5.1 %all-to-all-done.3 = bf16[16,8,512]{2,1,0:T(8,128)(2,1)S(1)} async-done(((bf16[16,8,512]{2,1,0:T(8,128)(2,1)}), bf16[16,8,512]{2,1,0:T(8,128)(2,1)S(1)}, u32[]{:S(2)}, u32[]{:S(2)}) %all-to-all-start.3) | async-done | bytes 131104 | tf_op jit(solution)/shard_map/all_to_all | solution.py:283
  79.2 0.0 copy-done.5
  79.2 2.2 %shard_map.126 = bf16[128,3712]{1,0:T(8,128)(2,1)S(1)} custom-call(bf16[128,512]{1,0:T(8,128)(2,1)S(1)} %bitcast.12, f32[1,512]{1,0:T(1,128)S(1)} %bitcast.15, bf16[512,896]{1,0:T(8,128)(2,1)S(1)} %copy-done.1, bf16[512,896]{1,0:T(8,128)(2,1)} %collective-permute-done.1.rest_1_, bf16[512,896]{1,0:T(8,128)(2,1)} %rest_2_.1, ...), custom_call_target="tpu_custom_call" | custom-call | flops 469762048 | bytes 3670016 | tf_op jit(solution)/shard_map/pallas_call | solution.py:343
  81.4 17.3 %all_to_all.35.parts_ref = bf16[16,8,3712]{2,1,0:T(8,128)(2,1)S(1)} all-to-all(bf16[16,8,3712]{2,1,0:T(8,128)(2,1)S(1)} %bitcast.10), channel_id=1, replica_groups={{260,261,262,263,0,1,2,3,4,5,6,7,256,257,258,259},{268,269,270,271,8,9,..., dimensions={0} | all-to-all | bytes 1900544 | tf_op jit(solution)/shard_map/all_to_all | solution.py:286
  98.7 0.2 shard_map.127
  98.9 12.7 %all_to_all.36 = bf16[16,8,1792]{2,1,0:T(8,128)(2,1)S(1)} all-to-all(bf16[16,8,1792]{2,1,0:T(8,128)(2,1)S(1)} %shard_map.127), channel_id=1, replica_groups={{260,261,262,263,0,1,2,3,4,5,6,7,256,257,258,259},{268,269,270,271,8,9,..., dimensions={0} | all-to-all | bytes 917504 | tf_op jit(solution)/shard_map/all_to_all | solution.py:286
  111.5 0.4 shard_map.128
  112.0 0.0 copy-start.4
  112.0 17.0 %all_to_all.37.parts_ref = bf16[16,8,512]{2,1,0:T(8,128)(2,1)S(1)} all-to-all(bf16[16,8,512]{2,1,0:T(8,128)(2,1)S(1)} %bitcast.13), channel_id=1, replica_groups={{128,144,160,176,192,208,224,240,0,16,32,48,64,80,96,112},{136,152,168,..., dimensions={0} | all-to-all | bytes 262144 | tf_op jit(solution)/shard_map/all_to_all | solution.py:283
  129.0 0.0 copy-done.4
  129.0 0.6 shard_map.129
Async XLA Ops:
  1.3 13.0 %copy-start.2 = (bf16[256,512]{1,0:T(8,128)(2,1)S(1)}, bf16[256,512]{1,0:T(8,128)(2,1)}, u32[]{:S(2)}) copy-start(bf16[256,512]{1,0:T(8,128)(2,1)} %mine_ref.2) | copy-start | bytes 786436
  4.1 33.1 %copy-start.1 = (bf16[512,896]{1,0:T(8,128)(2,1)S(1)}, bf16[512,896]{1,0:T(8,128)(2,1)}, u32[]{:S(2)}) copy-start(bf16[512,896]{1,0:T(8,128)(2,1)} %rest_0_.1) | copy-start | bytes 2752516
  4.2 16.4 %all-to-all-start = ((bf16[16,8,1152]{2,1,0:T(8,128)(2,1)}), bf16[16,8,1152]{2,1,0:T(8,128)(2,1)S(1)}, u32[]{:S(2)}, u32[]{:S(2)}) async-start(bf16[16,8,1152]{2,1,0:T(8,128)(2,1)} %shard_map.122), calls=%async_computation | async-start | bytes 589824 | tf_op jit(solution)/shard_map/all_to_all | solution.py:286
  14.3 41.6 %copy-start = (bf16[896,512]{1,0:T(8,128)(2,1)S(1)}, bf16[896,512]{1,0:T(8,128)(2,1)}, u32[]{:S(2)}) copy-start(bf16[896,512]{1,0:T(8,128)(2,1)} %mine_ref.3) | copy-start | bytes 2752516
  14.3 3.6 %collective-permute-start = (bf16[256,512]{1,0:T(8,128)(2,1)S(1)}, bf16[256,512]{1,0:T(8,128)(2,1)S(1)}, u32[]{:S(2)}, u32[]{:S(2)}) collective-permute-start(bf16[256,512]{1,0:T(8,128)(2,1)S(1)} %copy-done.2), channel_id=1, source_target_pairs={{0,8},{8,0},{16,24},{24,16},{32,40},{40,32},{48,56},{56,48},{64,72... | collective-permute-start | bytes 786440 | tf_op jit(solution)/shard_map/ppermute | solution.py:280
  21.5 21.3 %all-to-all-start.1 = ((bf16[16,8,512]{2,1,0:T(8,128)(2,1)}), bf16[16,8,512]{2,1,0:T(8,128)(2,1)S(1)}, u32[]{:S(2)}, u32[]{:S(2)}) async-start(bf16[16,8,512]{2,1,0:T(8,128)(2,1)} %shard_map.123), calls=%async_computation.1 | async-start | bytes 262144 | tf_op jit(solution)/shard_map/all_to_all | solution.py:283
  37.3 20.5 %collective-permute-start.1 = (bf16[512,896]{1,0:T(8,128)(2,1)S(1)}, bf16[512,896]{1,0:T(8,128)(2,1)}, u32[]{:S(2)}, u32[]{:S(2)}) collective-permute-start(bf16[512,896]{1,0:T(8,128)(2,1)S(1)} %copy-done.1), channel_id=1, source_target_pairs={{0,8},{8,0},{16,24},{24,16},{32,40},{40,32},{48,56},{56,48},{64,72... | collective-permute-start | bytes 2752520 | tf_op jit(solution)/shard_map/ppermute | solution.py:280
  39.2 18.6 %collective-permute-start.2 = (bf16[512,896]{1,0:T(8,128)(2,1)}, bf16[512,896]{1,0:T(8,128)(2,1)}, u32[]{:S(2)}, u32[]{:S(2)}) collective-permute-start(bf16[512,896]{1,0:T(8,128)(2,1)} %rest_2_.1), channel_id=1, source_target_pairs={{0,8},{8,0},{16,24},{24,16},{32,40},{40,32},{48,56},{56,48},{64,72... | collective-permute-start | bytes 2752520 | tf_op jit(solution)/shard_map/ppermute | solution.py:280
  43.7 17.7 %copy-start.3 = (bf16[8,512]{1,0:T(8,128)(2,1)S(1)}, bf16[8,512]{1,0:T(8,128)(2,1)}, u32[]{:S(2)}) copy-start(bf16[8,512]{1,0:T(8,128)(2,1)} %stream_ref.1) | copy-start | bytes 24580
  43.7 17.7 %all-to-all-start.2 = ((bf16[16,8,512]{2,1,0:T(8,128)(2,1)}), bf16[16,8,512]{2,1,0:T(8,128)(2,1)S(1)}, u32[]{:S(2)}, u32[]{:S(2)}) async-start(bf16[16,8,512]{2,1,0:T(8,128)(2,1)} %bitcast.3), calls=%async_computation.2 | async-start | bytes 262144 | tf_op jit(solution)/shard_map/all_to_all | solution.py:283
  55.9 18.3 %collective-permute-start.3 = (bf16[896,512]{1,0:T(8,128)(2,1)S(1)}, bf16[896,512]{1,0:T(8,128)(2,1)S(1)}, u32[]{:S(2)}, u32[]{:S(2)}) collective-permute-start(bf16[896,512]{1,0:T(8,128)(2,1)S(1)} %copy-done), channel_id=1, source_target_pairs={{0,8},{8,0},{16,24},{24,16},{32,40},{40,32},{48,56},{56,48},{64,72... | collective-permute-start | bytes 2752520 | tf_op jit(solution)/shard_map/ppermute | solution.py:280
  62.1 17.1 %all-to-all-start.3 = ((bf16[16,8,512]{2,1,0:T(8,128)(2,1)}), bf16[16,8,512]{2,1,0:T(8,128)(2,1)S(1)}, u32[]{:S(2)}, u32[]{:S(2)}) async-start(bf16[16,8,512]{2,1,0:T(8,128)(2,1)} %get-tuple-element.15), calls=%async_computation.3 | async-start | bytes 262144 | tf_op jit(solution)/shard_map/all_to_all | solution.py:283
  74.1 5.1 %copy-start.5 = (f32[512]{0:T(512)S(1)}, f32[512]{0:T(512)}, u32[]{:S(2)}) copy-start(f32[512]{0:T(512)} %param.18) | copy-start | bytes 6148
  112.0 17.0 %copy-start.4 = (bf16[8,512]{1,0:T(8,128)(2,1)S(1)}, bf16[8,512]{1,0:T(8,128)(2,1)}, u32[]{:S(2)}) copy-start(bf16[8,512]{1,0:T(8,128)(2,1)} %get-tuple-element.9.attended_ref) | copy-start | bytes 24580

commit v4 on v3

--- a/solution.py
+++ b/solution.py
@@ -75,7 +75,7 @@
         for part in range(2)
         for k in range(pieces)
     ]
-    for copy in small + large:
+    for copy in large[:pieces] + small + large[pieces:]:
         copy.start()
     for copy in small:
         copy.wait()
@@ -264,7 +264,7 @@
     cols = lax.axis_size("col")
     plane = lax.axis_size("grp") * cols
     chips = rows // 2
-    far = chips // 2
+    far = 5 * chips // 8
     targets = [(z + far) % chips for z in range(chips)]
     ring = [[2 * z + core for z in targets] for core in range(2)]
     sources = [(p + 12) % plane for p in range(plane)]
@@ -291,7 +291,7 @@
     other_down = swapped(down_weight)
 
     width = group * HD
-    pieces = 2
+    pieces = 1
     lines = call(
         functools.partial(attend_kernel, nodes, group, pieces),
         shape(plane, nodes, width + LANES),
@@ -348,7 +348,7 @@
         gate_weight.size * 8,
         scratch_shapes=[
             pltpu.VMEM((3,) + up_weight.shape, BF),
-            pltpu.SemaphoreType.DMA((3, 2)),
+            pltpu.SemaphoreType.DMA((3, 1)),
         ],
     )(mine, norm_gain.reshape(1, local), gate_weight, other_gate, up_weight, other_up)
     share = tokens // plane

time: 130 us -> 130 us (level)
  waiting for transfers between devices: 14 us -> 19.2 us
  starting transfers between devices: 58.4 us -> 53.2 us
    all_to_all x3, starting transfers between devices: 40 us -> 34.7 us  [along_ring(): return lax.all_to_all(x, 'row', 0, 0, axis_index_groups=ring, tiled=True)]
    all_to_all x3, waiting for transfers between devices: 9.84 us -> 15 us  [along_ring(): return lax.all_to_all(x, 'row', 0, 0, axis_index_groups=ring, tiled=True)]
where the time goes in v4:
time: 130 us; the launch traced here: 129 us
  starting transfers between devices  53.2 us (41%)
  blocking collectives  46.4 us (36%)
  waiting for transfers between devices  19.2 us (15%)
  Pallas kernels  8.84 us (7%)
  between operations  1.43 us (1%)
    all_to_all x3, starting transfers between devices, along_ring(): return lax.all_to_all(x, 'row', 0, 0, axis_index_groups=ring, tiled=True)  34.7 us
    all_to_all x2, blocking collectives, in_plane(): lax.all_to_all(x, PLANE, 0, 0, axis_index_groups=[sources], tiled=True)  29.2 us
    all_to_all x1, blocking collectives, along_ring(): return lax.all_to_all(x, 'row', 0, 0, axis_index_groups=ring, tiled=True)  17.2 us
    all_to_all x3, waiting for transfers between devices, along_ring(): return lax.all_to_all(x, 'row', 0, 0, axis_index_groups=ring, tiled=True)  15 us
    all_to_all x1, starting transfers between devices, in_plane(): lax.all_to_all(x, PLANE, 0, 0, axis_index_groups=[sources], tiled=True)  10.1 us
    ppermute x4, starting transfers between devices, swapped(): return lax.ppermute(x, 'row', swap)  8.3 us
    pallas_call x1, Pallas kernels, on_device(): call(functools.partial(attend_kernel, nodes, group, pieces), shape(plane,...  2.75 us
    all_to_all x1, waiting for transfers between devices, in_plane(): lax.all_to_all(x, PLANE, 0, 0, axis_index_groups=[sources], tiled=True)  2.71 us
  transfers between devices with their start and end apart: 8, of which 5 were waited for; matrix products, arithmetic and copies ran while one was open for 0% of the time, Pallas kernels for 1%

profile of v4, /device:TPU:16, one launch (start us, length us, event | category | flops | bytes accessed | tf_op | source)
XLA Modules:
  0.0 129.1 jit_solution(9044592309629714520)
XLA Ops:
  1.3 0.0 copy-start.2
  1.3 2.8 %shard_map.122 = bf16[16,8,1152]{2,1,0:T(8,128)(2,1)} custom-call(s32[1,1]{1,0:T(1,128)} %bitcast.9.length_ref, s32[1,8]{1,0:T(1,128)} %parents_ref.1, bf16[1,8,1024]{2,1,0:T(8,128)(2,1)} %q_ref.1, bf16[1,8,2,128]{3,2,1,0:T(2,128)(2,1)} %tree_ref.1, bf16[1,2,2048,128]{3,2,1,0:T(8,128)(2,1)} %cache_ref.1), custom_call_target="tpu_custom_call" | custom-call | flops 67108864 | bytes 1048576 | tf_op jit(solution)/shard_map/pallas_call | solution.py:295
  4.0 0.0 copy-start.1
  4.1 10.1 %all-to-all-start = ((bf16[16,8,1152]{2,1,0:T(8,128)(2,1)}), bf16[16,8,1152]{2,1,0:T(8,128)(2,1)S(1)}, u32[]{:S(2)}, u32[]{:S(2)}) async-start(bf16[16,8,1152]{2,1,0:T(8,128)(2,1)} %shard_map.122), calls=%async_computation | async-start | bytes 589824 | tf_op jit(solution)/shard_map/all_to_all | solution.py:286
  14.2 0.0 copy-done.2
  14.2 0.0 copy-start
  14.2 2.1 %collective-permute-start = (bf16[256,512]{1,0:T(8,128)(2,1)S(1)}, bf16[256,512]{1,0:T(8,128)(2,1)S(1)}, u32[]{:S(2)}, u32[]{:S(2)}) collective-permute-start(bf16[256,512]{1,0:T(8,128)(2,1)S(1)} %copy-done.2), channel_id=1, source_target_pairs={{0,8},{8,0},{16,24},{24,16},{32,40},{40,32},{48,56},{56,48},{64,72... | collective-permute-start | bytes 786440 | tf_op jit(solution)/shard_map/ppermute | solution.py:280
  16.3 1.5 %collective-permute-done.other_ref = bf16[256,512]{1,0:T(8,128)(2,1)S(1)} collective-permute-done((bf16[256,512]{1,0:T(8,128)(2,1)S(1)}, bf16[256,512]{1,0:T(8,128)(2,1)S(1)}, u32[]{:S(2)}, u32[]{:S(2)}) %collective-permute-start) | collective-permute-done | bytes 262176 | tf_op jit(solution)/shard_map/ppermute | solution.py:280
  17.8 2.7 %all-to-all-done.in_ref = bf16[16,8,1152]{2,1,0:T(8,128)(2,1)S(1)} async-done(((bf16[16,8,1152]{2,1,0:T(8,128)(2,1)}), bf16[16,8,1152]{2,1,0:T(8,128)(2,1)S(1)}, u32[]{:S(2)}, u32[]{:S(2)}) %all-to-all-start) | async-done | bytes 294944 | tf_op jit(solution)/shard_map/all_to_all | solution.py:286
  20.5 0.9 shard_map.123
  21.4 14.0 %all-to-all-start.1 = ((bf16[16,8,512]{2,1,0:T(8,128)(2,1)}), bf16[16,8,512]{2,1,0:T(8,128)(2,1)S(1)}, u32[]{:S(2)}, u32[]{:S(2)}) async-start(bf16[16,8,512]{2,1,0:T(8,128)(2,1)} %shard_map.123), calls=%async_computation.1 | async-start | bytes 262144 | tf_op jit(solution)/shard_map/all_to_all | solution.py:283
  35.4 0.0 copy-done.1
  35.4 1.9 %collective-permute-start.1 = (bf16[512,896]{1,0:T(8,128)(2,1)S(1)}, bf16[512,896]{1,0:T(8,128)(2,1)}, u32[]{:S(2)}, u32[]{:S(2)}) collective-permute-start(bf16[512,896]{1,0:T(8,128)(2,1)S(1)} %copy-done.1), channel_id=1, source_target_pairs={{0,8},{8,0},{16,24},{24,16},{32,40},{40,32},{48,56},{56,48},{64,72... | collective-permute-start | bytes 2752520 | tf_op jit(solution)/shard_map/ppermute | solution.py:280
  37.3 2.4 %collective-permute-start.2 = (bf16[512,896]{1,0:T(8,128)(2,1)}, bf16[512,896]{1,0:T(8,128)(2,1)}, u32[]{:S(2)}, u32[]{:S(2)}) collective-permute-start(bf16[512,896]{1,0:T(8,128)(2,1)} %rest_2_.1), channel_id=1, source_target_pairs={{0,8},{8,0},{16,24},{24,16},{32,40},{40,32},{48,56},{56,48},{64,72... | collective-permute-start | bytes 2752520 | tf_op jit(solution)/shard_map/ppermute | solution.py:280
  39.7 2.9 %all-to-all-done.1 = bf16[16,8,512]{2,1,0:T(8,128)(2,1)S(1)} async-done(((bf16[16,8,512]{2,1,0:T(8,128)(2,1)}), bf16[16,8,512]{2,1,0:T(8,128)(2,1)S(1)}, u32[]{:S(2)}, u32[]{:S(2)}) %all-to-all-start.1) | async-done | bytes 131104 | tf_op jit(solution)/shard_map/all_to_all | solution.py:283
  42.6 0.9 shard_map.124
  43.5 0.0 copy-start.3
  43.5 10.4 %all-to-all-start.2 = ((bf16[16,8,512]{2,1,0:T(8,128)(2,1)}), bf16[16,8,512]{2,1,0:T(8,128)(2,1)S(1)}, u32[]{:S(2)}, u32[]{:S(2)}) async-start(bf16[16,8,512]{2,1,0:T(8,128)(2,1)} %bitcast.3), calls=%async_computation.2 | async-start | bytes 262144 | tf_op jit(solution)/shard_map/all_to_all | solution.py:283
  54.0 0.0 copy-done
  54.0 1.9 %collective-permute-start.3 = (bf16[896,512]{1,0:T(8,128)(2,1)S(1)}, bf16[896,512]{1,0:T(8,128)(2,1)S(1)}, u32[]{:S(2)}, u32[]{:S(2)}) collective-permute-start(bf16[896,512]{1,0:T(8,128)(2,1)S(1)} %copy-done), channel_id=1, source_target_pairs={{0,8},{8,0},{16,24},{24,16},{32,40},{40,32},{48,56},{56,48},{64,72... | collective-permute-start | bytes 2752520 | tf_op jit(solution)/shard_map/ppermute | solution.py:280
  55.9 0.0 collective-permute-done.1.rest_1_
  55.9 0.0 collective-permute-done.2.rest_3_
  55.9 5.3 %all-to-all-done.2.parts_ref = bf16[16,8,512]{2,1,0:T(8,128)(2,1)S(1)} async-done(((bf16[16,8,512]{2,1,0:T(8,128)(2,1)}), bf16[16,8,512]{2,1,0:T(8,128)(2,1)S(1)}, u32[]{:S(2)}, u32[]{:S(2)}) %all-to-all-start.2) | async-done | bytes 131104 | tf_op jit(solution)/shard_map/all_to_all | solution.py:283
  61.2 0.0 copy-done.3
  61.2 0.7 shard_map.125
  61.9 10.3 %all-to-all-start.3 = ((bf16[16,8,512]{2,1,0:T(8,128)(2,1)}), bf16[16,8,512]{2,1,0:T(8,128)(2,1)S(1)}, u32[]{:S(2)}, u32[]{:S(2)}) async-start(bf16[16,8,512]{2,1,0:T(8,128)(2,1)} %get-tuple-element.15), calls=%async_computation.3 | async-start | bytes 262144 | tf_op jit(solution)/shard_map/all_to_all | solution.py:283
  72.2 0.0 copy-start.5
  72.2 0.0 collective-permute-done.3.other_ref
  72.2 6.8 %all-to-all-done.3 = bf16[16,8,512]{2,1,0:T(8,128)(2,1)S(1)} async-done(((bf16[16,8,512]{2,1,0:T(8,128)(2,1)}), bf16[16,8,512]{2,1,0:T(8,128)(2,1)S(1)}, u32[]{:S(2)}, u32[]{:S(2)}) %all-to-all-start.3) | async-done | bytes 131104 | tf_op jit(solution)/shard_map/all_to_all | solution.py:283
  79.1 0.0 copy-done.5
  79.1 2.3 %shard_map.126 = bf16[128,3712]{1,0:T(8,128)(2,1)S(1)} custom-call(bf16[128,512]{1,0:T(8,128)(2,1)S(1)} %bitcast.12, f32[1,512]{1,0:T(1,128)S(1)} %bitcast.15, bf16[512,896]{1,0:T(8,128)(2,1)S(1)} %copy-done.1, bf16[512,896]{1,0:T(8,128)(2,1)} %collective-permute-done.1.rest_1_, bf16[512,896]{1,0:T(8,128)(2,1)} %rest_2_.1, ...), custom_call_target="tpu_custom_call" | custom-call | flops 469762048 | bytes 3670016 | tf_op jit(solution)/shard_map/pallas_call | solution.py:343
  81.4 16.5 %all_to_all.35.parts_ref = bf16[16,8,3712]{2,1,0:T(8,128)(2,1)S(1)} all-to-all(bf16[16,8,3712]{2,1,0:T(8,128)(2,1)S(1)} %bitcast.10), channel_id=1, replica_groups={{260,261,262,263,0,1,2,3,4,5,6,7,256,257,258,259},{268,269,270,271,8,9,..., dimensions={0} | all-to-all | bytes 1900544 | tf_op jit(solution)/shard_map/all_to_all | solution.py:286
  97.9 0.2 shard_map.127
  98.1 12.7 %all_to_all.36 = bf16[16,8,1792]{2,1,0:T(8,128)(2,1)S(1)} all-to-all(bf16[16,8,1792]{2,1,0:T(8,128)(2,1)S(1)} %shard_map.127), channel_id=1, replica_groups={{260,261,262,263,0,1,2,3,4,5,6,7,256,257,258,259},{268,269,270,271,8,9,..., dimensions={0} | all-to-all | bytes 917504 | tf_op jit(solution)/shard_map/all_to_all | solution.py:286
  110.7 0.4 shard_map.128
  111.2 0.0 copy-start.4
  111.2 17.2 %all_to_all.37.parts_ref = bf16[16,8,512]{2,1,0:T(8,128)(2,1)S(1)} all-to-all(bf16[16,8,512]{2,1,0:T(8,128)(2,1)S(1)} %bitcast.13), channel_id=1, replica_groups={{160,176,192,208,224,240,0,16,32,48,64,80,96,112,128,144},{168,184,200,..., dimensions={0} | all-to-all | bytes 262144 | tf_op jit(solution)/shard_map/all_to_all | solution.py:283
  128.5 0.0 copy-done.4
  128.5 0.6 shard_map.129
Async XLA Ops:
  1.3 12.9 %copy-start.2 = (bf16[256,512]{1,0:T(8,128)(2,1)S(1)}, bf16[256,512]{1,0:T(8,128)(2,1)}, u32[]{:S(2)}) copy-start(bf16[256,512]{1,0:T(8,128)(2,1)} %mine_ref.2) | copy-start | bytes 786436
  4.0 31.3 %copy-start.1 = (bf16[512,896]{1,0:T(8,128)(2,1)S(1)}, bf16[512,896]{1,0:T(8,128)(2,1)}, u32[]{:S(2)}) copy-start(bf16[512,896]{1,0:T(8,128)(2,1)} %rest_0_.1) | copy-start | bytes 2752516
  4.1 16.4 %all-to-all-start = ((bf16[16,8,1152]{2,1,0:T(8,128)(2,1)}), bf16[16,8,1152]{2,1,0:T(8,128)(2,1)S(1)}, u32[]{:S(2)}, u32[]{:S(2)}) async-start(bf16[16,8,1152]{2,1,0:T(8,128)(2,1)} %shard_map.122), calls=%async_computation | async-start | bytes 589824 | tf_op jit(solution)/shard_map/all_to_all | solution.py:286
  14.2 39.8 %copy-start = (bf16[896,512]{1,0:T(8,128)(2,1)S(1)}, bf16[896,512]{1,0:T(8,128)(2,1)}, u32[]{:S(2)}) copy-start(bf16[896,512]{1,0:T(8,128)(2,1)} %mine_ref.3) | copy-start | bytes 2752516
  14.2 3.6 %collective-permute-start = (bf16[256,512]{1,0:T(8,128)(2,1)S(1)}, bf16[256,512]{1,0:T(8,128)(2,1)S(1)}, u32[]{:S(2)}, u32[]{:S(2)}) collective-permute-start(bf16[256,512]{1,0:T(8,128)(2,1)S(1)} %copy-done.2), channel_id=1, source_target_pairs={{0,8},{8,0},{16,24},{24,16},{32,40},{40,32},{48,56},{56,48},{64,72... | collective-permute-start | bytes 786440 | tf_op jit(solution)/shard_map/ppermute | solution.py:280
  21.4 21.2 %all-to-all-start.1 = ((bf16[16,8,512]{2,1,0:T(8,128)(2,1)}), bf16[16,8,512]{2,1,0:T(8,128)(2,1)S(1)}, u32[]{:S(2)}, u32[]{:S(2)}) async-start(bf16[16,8,512]{2,1,0:T(8,128)(2,1)} %shard_map.123), calls=%async_computation.1 | async-start | bytes 262144 | tf_op jit(solution)/shard_map/all_to_all | solution.py:283
  35.4 20.5 %collective-permute-start.1 = (bf16[512,896]{1,0:T(8,128)(2,1)S(1)}, bf16[512,896]{1,0:T(8,128)(2,1)}, u32[]{:S(2)}, u32[]{:S(2)}) collective-permute-start(bf16[512,896]{1,0:T(8,128)(2,1)S(1)} %copy-done.1), channel_id=1, source_target_pairs={{0,8},{8,0},{16,24},{24,16},{32,40},{40,32},{48,56},{56,48},{64,72... | collective-permute-start | bytes 2752520 | tf_op jit(solution)/shard_map/ppermute | solution.py:280
  37.3 18.6 %collective-permute-start.2 = (bf16[512,896]{1,0:T(8,128)(2,1)}, bf16[512,896]{1,0:T(8,128)(2,1)}, u32[]{:S(2)}, u32[]{:S(2)}) collective-permute-start(bf16[512,896]{1,0:T(8,128)(2,1)} %rest_2_.1), channel_id=1, source_target_pairs={{0,8},{8,0},{16,24},{24,16},{32,40},{40,32},{48,56},{56,48},{64,72... | collective-permute-start | bytes 2752520 | tf_op jit(solution)/shard_map/ppermute | solution.py:280
  43.5 17.7 %copy-start.3 = (bf16[8,512]{1,0:T(8,128)(2,1)S(1)}, bf16[8,512]{1,0:T(8,128)(2,1)}, u32[]{:S(2)}) copy-start(bf16[8,512]{1,0:T(8,128)(2,1)} %stream_ref.1) | copy-start | bytes 24580
  43.5 17.7 %all-to-all-start.2 = ((bf16[16,8,512]{2,1,0:T(8,128)(2,1)}), bf16[16,8,512]{2,1,0:T(8,128)(2,1)S(1)}, u32[]{:S(2)}, u32[]{:S(2)}) async-start(bf16[16,8,512]{2,1,0:T(8,128)(2,1)} %bitcast.3), calls=%async_computation.2 | async-start | bytes 262144 | tf_op jit(solution)/shard_map/all_to_all | solution.py:283
  54.0 18.3 %collective-permute-start.3 = (bf16[896,512]{1,0:T(8,128)(2,1)S(1)}, bf16[896,512]{1,0:T(8,128)(2,1)S(1)}, u32[]{:S(2)}, u32[]{:S(2)}) collective-permute-start(bf16[896,512]{1,0:T(8,128)(2,1)S(1)} %copy-done), channel_id=1, source_target_pairs={{0,8},{8,0},{16,24},{24,16},{32,40},{40,32},{48,56},{56,48},{64,72... | collective-permute-start | bytes 2752520 | tf_op jit(solution)/shard_map/ppermute | solution.py:280
  61.9 17.2 %all-to-all-start.3 = ((bf16[16,8,512]{2,1,0:T(8,128)(2,1)}), bf16[16,8,512]{2,1,0:T(8,128)(2,1)S(1)}, u32[]{:S(2)}, u32[]{:S(2)}) async-start(bf16[16,8,512]{2,1,0:T(8,128)(2,1)} %get-tuple-element.15), calls=%async_computation.3 | async-start | bytes 262144 | tf_op jit(solution)/shard_map/all_to_all | solution.py:283
  72.2 6.8 %copy-start.5 = (f32[512]{0:T(512)S(1)}, f32[512]{0:T(512)}, u32[]{:S(2)}) copy-start(f32[512]{0:T(512)} %param.18) | copy-start | bytes 6148
  111.2 17.3 %copy-start.4 = (bf16[8,512]{1,0:T(8,128)(2,1)S(1)}, bf16[8,512]{1,0:T(8,128)(2,1)}, u32[]{:S(2)}) copy-start(bf16[8,512]{1,0:T(8,128)(2,1)} %get-tuple-element.9.attended_ref) | copy-start | bytes 24580

commit v5 on v4

--- a/solution.py
+++ b/solution.py
@@ -348,7 +348,7 @@
         gate_weight.size * 8,
         scratch_shapes=[
             pltpu.VMEM((3,) + up_weight.shape, BF),
-            pltpu.SemaphoreType.DMA((3, 1)),
+            pltpu.SemaphoreType.DMA((3, 2)),
         ],
     )(mine, norm_gain.reshape(1, local), gate_weight, other_gate, up_weight, other_up)
     share = tokens // plane

time: 130 us -> 130 us (level)
  no operation moved by 1% of the time
where the time goes in v5:
time: 130 us; the launch traced here: 129 us
  starting transfers between devices  53.2 us (41%)
  blocking collectives  46.4 us (36%)
  waiting for transfers between devices  19.2 us (15%)
  Pallas kernels  8.69 us (7%)
  between operations  1.43 us (1%)
    all_to_all x3, starting transfers between devices, along_ring(): return lax.all_to_all(x, 'row', 0, 0, axis_index_groups=ring, tiled=True)  34.7 us
    all_to_all x2, blocking collectives, in_plane(): lax.all_to_all(x, PLANE, 0, 0, axis_index_groups=[sources], tiled=True)  29.2 us
    all_to_all x1, blocking collectives, along_ring(): return lax.all_to_all(x, 'row', 0, 0, axis_index_groups=ring, tiled=True)  17.3 us
    all_to_all x3, waiting for transfers between devices, along_ring(): return lax.all_to_all(x, 'row', 0, 0, axis_index_groups=ring, tiled=True)  15 us
    all_to_all x1, starting transfers between devices, in_plane(): lax.all_to_all(x, PLANE, 0, 0, axis_index_groups=[sources], tiled=True)  10.1 us
    ppermute x4, starting transfers between devices, swapped(): return lax.ppermute(x, 'row', swap)  8.3 us
    pallas_call x1, Pallas kernels, on_device(): call(functools.partial(attend_kernel, nodes, group, pieces), shape(plane,...  2.75 us
    all_to_all x1, waiting for transfers between devices, in_plane(): lax.all_to_all(x, PLANE, 0, 0, axis_index_groups=[sources], tiled=True)  2.71 us
  transfers between devices with their start and end apart: 8, of which 5 were waited for; matrix products, arithmetic and copies ran while one was open for 0% of the time, Pallas kernels for 1%

profile of v5, /device:TPU:16, one launch (start us, length us, event | category | flops | bytes accessed | tf_op | source)
XLA Modules:
  0.0 128.9 jit_solution(1871475774889924379)
XLA Ops:
  1.3 0.0 copy-start.2
  1.3 2.8 %shard_map.122 = bf16[16,8,1152]{2,1,0:T(8,128)(2,1)} custom-call(s32[1,1]{1,0:T(1,128)} %bitcast.9.length_ref, s32[1,8]{1,0:T(1,128)} %parents_ref.1, bf16[1,8,1024]{2,1,0:T(8,128)(2,1)} %q_ref.1, bf16[1,8,2,128]{3,2,1,0:T(2,128)(2,1)} %tree_ref.1, bf16[1,2,2048,128]{3,2,1,0:T(8,128)(2,1)} %cache_ref.1), custom_call_target="tpu_custom_call" | custom-call | flops 67108864 | bytes 1048576 | tf_op jit(solution)/shard_map/pallas_call | solution.py:295
  4.0 0.0 copy-start.1
  4.1 10.1 %all-to-all-start = ((bf16[16,8,1152]{2,1,0:T(8,128)(2,1)}), bf16[16,8,1152]{2,1,0:T(8,128)(2,1)S(1)}, u32[]{:S(2)}, u32[]{:S(2)}) async-start(bf16[16,8,1152]{2,1,0:T(8,128)(2,1)} %shard_map.122), calls=%async_computation | async-start | bytes 589824 | tf_op jit(solution)/shard_map/all_to_all | solution.py:286
  14.2 0.0 copy-done.2
  14.2 0.0 copy-start
  14.2 2.1 %collective-permute-start = (bf16[256,512]{1,0:T(8,128)(2,1)S(1)}, bf16[256,512]{1,0:T(8,128)(2,1)S(1)}, u32[]{:S(2)}, u32[]{:S(2)}) collective-permute-start(bf16[256,512]{1,0:T(8,128)(2,1)S(1)} %copy-done.2), channel_id=1, source_target_pairs={{0,8},{8,0},{16,24},{24,16},{32,40},{40,32},{48,56},{56,48},{64,72... | collective-permute-start | bytes 786440 | tf_op jit(solution)/shard_map/ppermute | solution.py:280
  16.3 1.5 %collective-permute-done.other_ref = bf16[256,512]{1,0:T(8,128)(2,1)S(1)} collective-permute-done((bf16[256,512]{1,0:T(8,128)(2,1)S(1)}, bf16[256,512]{1,0:T(8,128)(2,1)S(1)}, u32[]{:S(2)}, u32[]{:S(2)}) %collective-permute-start) | collective-permute-done | bytes 262176 | tf_op jit(solution)/shard_map/ppermute | solution.py:280
  17.8 2.7 %all-to-all-done.in_ref = bf16[16,8,1152]{2,1,0:T(8,128)(2,1)S(1)} async-done(((bf16[16,8,1152]{2,1,0:T(8,128)(2,1)}), bf16[16,8,1152]{2,1,0:T(8,128)(2,1)S(1)}, u32[]{:S(2)}, u32[]{:S(2)}) %all-to-all-start) | async-done | bytes 294944 | tf_op jit(solution)/shard_map/all_to_all | solution.py:286
  20.5 0.9 shard_map.123
  21.4 14.0 %all-to-all-start.1 = ((bf16[16,8,512]{2,1,0:T(8,128)(2,1)}), bf16[16,8,512]{2,1,0:T(8,128)(2,1)S(1)}, u32[]{:S(2)}, u32[]{:S(2)}) async-start(bf16[16,8,512]{2,1,0:T(8,128)(2,1)} %shard_map.123), calls=%async_computation.1 | async-start | bytes 262144 | tf_op jit(solution)/shard_map/all_to_all | solution.py:283
  35.4 0.0 copy-done.1
  35.4 1.9 %collective-permute-start.1 = (bf16[512,896]{1,0:T(8,128)(2,1)S(1)}, bf16[512,896]{1,0:T(8,128)(2,1)}, u32[]{:S(2)}, u32[]{:S(2)}) collective-permute-start(bf16[512,896]{1,0:T(8,128)(2,1)S(1)} %copy-done.1), channel_id=1, source_target_pairs={{0,8},{8,0},{16,24},{24,16},{32,40},{40,32},{48,56},{56,48},{64,72... | collective-permute-start | bytes 2752520 | tf_op jit(solution)/shard_map/ppermute | solution.py:280
  37.3 2.4 %collective-permute-start.2 = (bf16[512,896]{1,0:T(8,128)(2,1)}, bf16[512,896]{1,0:T(8,128)(2,1)}, u32[]{:S(2)}, u32[]{:S(2)}) collective-permute-start(bf16[512,896]{1,0:T(8,128)(2,1)} %rest_2_.1), channel_id=1, source_target_pairs={{0,8},{8,0},{16,24},{24,16},{32,40},{40,32},{48,56},{56,48},{64,72... | collective-permute-start | bytes 2752520 | tf_op jit(solution)/shard_map/ppermute | solution.py:280
  39.7 2.9 %all-to-all-done.1 = bf16[16,8,512]{2,1,0:T(8,128)(2,1)S(1)} async-done(((bf16[16,8,512]{2,1,0:T(8,128)(2,1)}), bf16[16,8,512]{2,1,0:T(8,128)(2,1)S(1)}, u32[]{:S(2)}, u32[]{:S(2)}) %all-to-all-start.1) | async-done | bytes 131104 | tf_op jit(solution)/shard_map/all_to_all | solution.py:283
  42.6 0.9 shard_map.124
  43.5 0.0 copy-start.3
  43.5 10.4 %all-to-all-start.2 = ((bf16[16,8,512]{2,1,0:T(8,128)(2,1)}), bf16[16,8,512]{2,1,0:T(8,128)(2,1)S(1)}, u32[]{:S(2)}, u32[]{:S(2)}) async-start(bf16[16,8,512]{2,1,0:T(8,128)(2,1)} %bitcast.3), calls=%async_computation.2 | async-start | bytes 262144 | tf_op jit(solution)/shard_map/all_to_all | solution.py:283
  54.0 0.0 copy-done
  54.0 1.9 %collective-permute-start.3 = (bf16[896,512]{1,0:T(8,128)(2,1)S(1)}, bf16[896,512]{1,0:T(8,128)(2,1)S(1)}, u32[]{:S(2)}, u32[]{:S(2)}) collective-permute-start(bf16[896,512]{1,0:T(8,128)(2,1)S(1)} %copy-done), channel_id=1, source_target_pairs={{0,8},{8,0},{16,24},{24,16},{32,40},{40,32},{48,56},{56,48},{64,72... | collective-permute-start | bytes 2752520 | tf_op jit(solution)/shard_map/ppermute | solution.py:280
  55.9 0.0 collective-permute-done.1.rest_1_
  55.9 0.0 collective-permute-done.2.rest_3_
  55.9 5.3 %all-to-all-done.2.parts_ref = bf16[16,8,512]{2,1,0:T(8,128)(2,1)S(1)} async-done(((bf16[16,8,512]{2,1,0:T(8,128)(2,1)}), bf16[16,8,512]{2,1,0:T(8,128)(2,1)S(1)}, u32[]{:S(2)}, u32[]{:S(2)}) %all-to-all-start.2) | async-done | bytes 131104 | tf_op jit(solution)/shard_map/all_to_all | solution.py:283
  61.2 0.0 copy-done.3
  61.2 0.7 shard_map.125
  61.9 10.3 %all-to-all-start.3 = ((bf16[16,8,512]{2,1,0:T(8,128)(2,1)}), bf16[16,8,512]{2,1,0:T(8,128)(2,1)S(1)}, u32[]{:S(2)}, u32[]{:S(2)}) async-start(bf16[16,8,512]{2,1,0:T(8,128)(2,1)} %get-tuple-element.15), calls=%async_computation.3 | async-start | bytes 262144 | tf_op jit(solution)/shard_map/all_to_all | solution.py:283
  72.2 0.0 copy-start.5
  72.2 0.0 collective-permute-done.3.other_ref
  72.2 6.8 %all-to-all-done.3 = bf16[16,8,512]{2,1,0:T(8,128)(2,1)S(1)} async-done(((bf16[16,8,512]{2,1,0:T(8,128)(2,1)}), bf16[16,8,512]{2,1,0:T(8,128)(2,1)S(1)}, u32[]{:S(2)}, u32[]{:S(2)}) %all-to-all-start.3) | async-done | bytes 131104 | tf_op jit(solution)/shard_map/all_to_all | solution.py:283
  79.1 0.0 copy-done.5
  79.1 2.2 %shard_map.126 = bf16[128,3712]{1,0:T(8,128)(2,1)S(1)} custom-call(bf16[128,512]{1,0:T(8,128)(2,1)S(1)} %bitcast.12, f32[1,512]{1,0:T(1,128)S(1)} %bitcast.15, bf16[512,896]{1,0:T(8,128)(2,1)S(1)} %copy-done.1, bf16[512,896]{1,0:T(8,128)(2,1)} %collective-permute-done.1.rest_1_, bf16[512,896]{1,0:T(8,128)(2,1)} %rest_2_.1, ...), custom_call_target="tpu_custom_call" | custom-call | flops 469762048 | bytes 3670016 | tf_op jit(solution)/shard_map/pallas_call | solution.py:343
  81.2 16.5 %all_to_all.35.parts_ref = bf16[16,8,3712]{2,1,0:T(8,128)(2,1)S(1)} all-to-all(bf16[16,8,3712]{2,1,0:T(8,128)(2,1)S(1)} %bitcast.10), channel_id=1, replica_groups={{260,261,262,263,0,1,2,3,4,5,6,7,256,257,258,259},{268,269,270,271,8,9,..., dimensions={0} | all-to-all | bytes 1900544 | tf_op jit(solution)/shard_map/all_to_all | solution.py:286
  97.8 0.2 shard_map.127
  98.0 12.6 %all_to_all.36 = bf16[16,8,1792]{2,1,0:T(8,128)(2,1)S(1)} all-to-all(bf16[16,8,1792]{2,1,0:T(8,128)(2,1)S(1)} %shard_map.127), channel_id=1, replica_groups={{260,261,262,263,0,1,2,3,4,5,6,7,256,257,258,259},{268,269,270,271,8,9,..., dimensions={0} | all-to-all | bytes 917504 | tf_op jit(solution)/shard_map/all_to_all | solution.py:286
  110.6 0.4 shard_map.128
  111.0 0.0 copy-start.4
  111.1 17.3 %all_to_all.37.parts_ref = bf16[16,8,512]{2,1,0:T(8,128)(2,1)S(1)} all-to-all(bf16[16,8,512]{2,1,0:T(8,128)(2,1)S(1)} %bitcast.13), channel_id=1, replica_groups={{160,176,192,208,224,240,0,16,32,48,64,80,96,112,128,144},{168,184,200,..., dimensions={0} | all-to-all | bytes 262144 | tf_op jit(solution)/shard_map/all_to_all | solution.py:283
  128.3 0.0 copy-done.4
  128.3 0.6 shard_map.129
Async XLA Ops:
  1.3 12.9 %copy-start.2 = (bf16[256,512]{1,0:T(8,128)(2,1)S(1)}, bf16[256,512]{1,0:T(8,128)(2,1)}, u32[]{:S(2)}) copy-start(bf16[256,512]{1,0:T(8,128)(2,1)} %mine_ref.2) | copy-start | bytes 786436
  4.0 31.3 %copy-start.1 = (bf16[512,896]{1,0:T(8,128)(2,1)S(1)}, bf16[512,896]{1,0:T(8,128)(2,1)}, u32[]{:S(2)}) copy-start(bf16[512,896]{1,0:T(8,128)(2,1)} %rest_0_.1) | copy-start | bytes 2752516
  4.1 16.4 %all-to-all-start = ((bf16[16,8,1152]{2,1,0:T(8,128)(2,1)}), bf16[16,8,1152]{2,1,0:T(8,128)(2,1)S(1)}, u32[]{:S(2)}, u32[]{:S(2)}) async-start(bf16[16,8,1152]{2,1,0:T(8,128)(2,1)} %shard_map.122), calls=%async_computation | async-start | bytes 589824 | tf_op jit(solution)/shard_map/all_to_all | solution.py:286
  14.2 39.8 %copy-start = (bf16[896,512]{1,0:T(8,128)(2,1)S(1)}, bf16[896,512]{1,0:T(8,128)(2,1)}, u32[]{:S(2)}) copy-start(bf16[896,512]{1,0:T(8,128)(2,1)} %mine_ref.3) | copy-start | bytes 2752516
  14.2 3.6 %collective-permute-start = (bf16[256,512]{1,0:T(8,128)(2,1)S(1)}, bf16[256,512]{1,0:T(8,128)(2,1)S(1)}, u32[]{:S(2)}, u32[]{:S(2)}) collective-permute-start(bf16[256,512]{1,0:T(8,128)(2,1)S(1)} %copy-done.2), channel_id=1, source_target_pairs={{0,8},{8,0},{16,24},{24,16},{32,40},{40,32},{48,56},{56,48},{64,72... | collective-permute-start | bytes 786440 | tf_op jit(solution)/shard_map/ppermute | solution.py:280
  21.4 21.2 %all-to-all-start.1 = ((bf16[16,8,512]{2,1,0:T(8,128)(2,1)}), bf16[16,8,512]{2,1,0:T(8,128)(2,1)S(1)}, u32[]{:S(2)}, u32[]{:S(2)}) async-start(bf16[16,8,512]{2,1,0:T(8,128)(2,1)} %shard_map.123), calls=%async_computation.1 | async-start | bytes 262144 | tf_op jit(solution)/shard_map/all_to_all | solution.py:283
  35.4 20.5 %collective-permute-start.1 = (bf16[512,896]{1,0:T(8,128)(2,1)S(1)}, bf16[512,896]{1,0:T(8,128)(2,1)}, u32[]{:S(2)}, u32[]{:S(2)}) collective-permute-start(bf16[512,896]{1,0:T(8,128)(2,1)S(1)} %copy-done.1), channel_id=1, source_target_pairs={{0,8},{8,0},{16,24},{24,16},{32,40},{40,32},{48,56},{56,48},{64,72... | collective-permute-start | bytes 2752520 | tf_op jit(solution)/shard_map/ppermute | solution.py:280
  37.3 18.6 %collective-permute-start.2 = (bf16[512,896]{1,0:T(8,128)(2,1)}, bf16[512,896]{1,0:T(8,128)(2,1)}, u32[]{:S(2)}, u32[]{:S(2)}) collective-permute-start(bf16[512,896]{1,0:T(8,128)(2,1)} %rest_2_.1), channel_id=1, source_target_pairs={{0,8},{8,0},{16,24},{24,16},{32,40},{40,32},{48,56},{56,48},{64,72... | collective-permute-start | bytes 2752520 | tf_op jit(solution)/shard_map/ppermute | solution.py:280
  43.5 17.7 %copy-start.3 = (bf16[8,512]{1,0:T(8,128)(2,1)S(1)}, bf16[8,512]{1,0:T(8,128)(2,1)}, u32[]{:S(2)}) copy-start(bf16[8,512]{1,0:T(8,128)(2,1)} %stream_ref.1) | copy-start | bytes 24580
  43.5 17.7 %all-to-all-start.2 = ((bf16[16,8,512]{2,1,0:T(8,128)(2,1)}), bf16[16,8,512]{2,1,0:T(8,128)(2,1)S(1)}, u32[]{:S(2)}, u32[]{:S(2)}) async-start(bf16[16,8,512]{2,1,0:T(8,128)(2,1)} %bitcast.3), calls=%async_computation.2 | async-start | bytes 262144 | tf_op jit(solution)/shard_map/all_to_all | solution.py:283
  54.0 18.3 %collective-permute-start.3 = (bf16[896,512]{1,0:T(8,128)(2,1)S(1)}, bf16[896,512]{1,0:T(8,128)(2,1)S(1)}, u32[]{:S(2)}, u32[]{:S(2)}) collective-permute-start(bf16[896,512]{1,0:T(8,128)(2,1)S(1)} %copy-done), channel_id=1, source_target_pairs={{0,8},{8,0},{16,24},{24,16},{32,40},{40,32},{48,56},{56,48},{64,72... | collective-permute-start | bytes 2752520 | tf_op jit(solution)/shard_map/ppermute | solution.py:280
  61.9 17.2 %all-to-all-start.3 = ((bf16[16,8,512]{2,1,0:T(8,128)(2,1)}), bf16[16,8,512]{2,1,0:T(8,128)(2,1)S(1)}, u32[]{:S(2)}, u32[]{:S(2)}) async-start(bf16[16,8,512]{2,1,0:T(8,128)(2,1)} %get-tuple-element.15), calls=%async_computation.3 | async-start | bytes 262144 | tf_op jit(solution)/shard_map/all_to_all | solution.py:283
  72.2 6.8 %copy-start.5 = (f32[512]{0:T(512)S(1)}, f32[512]{0:T(512)}, u32[]{:S(2)}) copy-start(f32[512]{0:T(512)} %param.18) | copy-start | bytes 6148
  111.0 17.3 %copy-start.4 = (bf16[8,512]{1,0:T(8,128)(2,1)S(1)}, bf16[8,512]{1,0:T(8,128)(2,1)}, u32[]{:S(2)}) copy-start(bf16[8,512]{1,0:T(8,128)(2,1)} %get-tuple-element.9.attended_ref) | copy-start | bytes 24580
